TPU v7x, 32 devices: a whole 2x2x4 slice. The times are simulated.
32 devices in a mesh: groups: 2 (over x), dp: 16 (over z, y, core).
Axes of the slice: x: 2, y: 2, z: 4, core: 2. Of those that a mesh axis runs over, the one named last changes fastest.
Arguments:
- hidden: bfloat16 [768, 4096], P(('groups', 'dp')), parts along dimension 0, may hold values from -6 to 6
- in_weight: bfloat16 [4096, 16384], P(None, 'dp'), may hold values from -0.09375 to 0.09375
- dt_weight: bfloat16 [32, 4096], P('dp'), may hold values from -0.09375 to 0.09375
- dt_bias: float32 [32], P('dp'), may hold values from -4 to -2
- decay_rate: float32 [32], P('dp'), may hold values from 0.003 to 0.5
- conv_weight: bfloat16 [4, 12288], P(None, 'dp'), may hold values from -3 to 3
- conv_bias: bfloat16 [12288], P('dp'), may hold values from -3 to 3
- skip: float32 [32], P('dp'), may hold values from 0.5 to 1.5
- norm_gain: bfloat16 [4096], P('dp'), may hold values from 0.099609375 to 1.8984375
- out_weight: bfloat16 [4096, 4096], P('dp'), may hold values from -0.09375 to 0.09375
- state_pool: bfloat16 [1024, 32, 128], P(('groups', 'dp')), parts along dimension 0, may hold values from -2 to 2
- conv_pool: bfloat16 [1024, 3, 96], P(('groups', 'dp')), parts along dimension 0, may hold values from -6 to 6
- hit_page: int32 [4, 32, 4], P('groups'), parts along dimension 0, may hold values from 0 to 511, as said below
- prefix_blocks: int32 [4], P('groups'), parts along dimension 0, may hold values from 1 to 2
- owners: int32 [32], P('groups'), parts along dimension 0, may hold values from 0 to 15, each once
Outputs:
- mixed: bfloat16 [768, 4096], P(('groups', 'dp')), parts along dimension 0
- final_state: float32 [4, 32, 128, 128], P('groups', 'dp'), parts along dimension 0
- final_conv: bfloat16 [4, 3, 12288], P('groups', None, 'dp'), parts along dimension 0
There are 2 independent parts, one for each index of `groups`. A program takes and returns all parts, laid end to end along the dimension named above; an argument that names none is the same for every part. Nothing has to cross between parts.
Inputs may be any that keep to these rules, and one draw needn't show every extreme that they name: All entries differ. Call rows d * 32 to d * 32 + 31 of the pools the block of holder d. For every index e of dp, of the entries hit_page[r, h, p] with h // 2 = e, at most 2 lie in the block of any one holder; in every draw some holder's block holds exactly 2 of them, and some block has all 32 of its rows named.
All inputs are finite; a program needn't handle non-finite values.
Results may differ from a plain program's by a relative error of at most 0.008.
Values may be sent and summed in bfloat16 or wider, within the bound.
No kernel may reach another device: no remote copies, remote signals or barrier semaphores. Data moves between devices by JAX's collectives and lax.ppermute only.
A program may use at most 64 MiB of HBM per device.

v0:
```python
import functools

import jax
import jax.numpy as jnp
from jax import lax
from jax.experimental import pallas as pl
from jax.experimental.pallas import tpu as pltpu
from jax.sharding import PartitionSpec as P

HEAD_DIM = 128
STATE = 128
CONV = 4
REQS = 2
SPAN = 192
BLK = 64


EPSILON = 1e-05
PER_PEER = 2
VMEM_LIMIT = 16 * 1024 * 1024
VMEM_ALL = 60 * 1024 * 1024


def folded(chip_count):
    return chip_count <= 8


def chip_at(place, chip_count):
    if not folded(chip_count):
        return place
    back = 2 * (chip_count - 1 - place) + 1
    if isinstance(place, int):
        return 2 * place if place < chip_count // 2 else back
    return jnp.where(place < chip_count // 2, 2 * place, back)


def place_of(chip, chip_count):
    if not folded(chip_count):
        return chip
    return jnp.where(chip % 2 == 0, chip // 2, chip_count - 1 - chip // 2)


def stream(array, chip_count):
    pairs = []
    for place in range(chip_count):
        for core in range(2):
            onto = (place + 1 - 2 * core) % chip_count
            pairs.append((2 * chip_at(place, chip_count) + core, 2 * chip_at(onto, chip_count) + core))
    return lax.ppermute(array, "dp", pairs)


def stream_other(array, chip_count):
    pairs = []
    for place in range(chip_count):
        for core in range(2):
            onto = (place + 1 - 2 * core) % chip_count
            pairs.append(
                (2 * chip_at(place, chip_count) + 1 - core, 2 * chip_at(onto, chip_count) + core)
            )
    return lax.ppermute(array, "dp", pairs)


def other_core(array, chip_count):
    return lax.ppermute(array, "dp", [(d, d ^ 1) for d in range(2 * chip_count)])


def kernel_call(kernel, outs, operands, scratch, name, flops=0, smem=0, limit=VMEM_LIMIT):
    several = isinstance(outs, list)
    whole = pl.BlockSpec(memory_space=pltpu.VMEM)
    scalars = pl.BlockSpec(memory_space=pltpu.SMEM)
    return pl.pallas_call(
        kernel,
        out_shape=outs,
        in_specs=[scalars] * smem + [whole] * (len(operands) - smem),
        out_specs=[whole] * len(outs) if several else whole,
        scratch_shapes=scratch,
        compiler_params=pltpu.CompilerParams(vmem_limit_bytes=limit),
        cost_estimate=pl.CostEstimate(flops=flops, bytes_accessed=8 << 20, transcendentals=0),
        name=name,
    )(*operands)


def offer_kernel(entries, my_ref, ids_ref, state_ref, conv_ref, out_ref, slot_s, conv_s, lag_s):
    pool_slots, state_rows, _ = state_ref.shape
    lag_rows = conv_ref.shape[0]
    piece_channels = conv_ref.shape[2]
    receivers = out_ref.shape[0]
    heads_dev = ids_ref.shape[2] // receivers
    first = my_ref[0] * pool_slots
    conv_s[...] = jnp.zeros_like(conv_s)
    conv_s[:, :, :piece_channels] = conv_ref[...].astype(jnp.float32)
    lag_s[...] = jnp.zeros_like(lag_s)

    def one_receiver(receiver, _):
        used = jnp.int32(0)
        for r in range(REQS):
            for h in range(heads_dev):
                for p in range(ids_ref.shape[1]):
                    slot = ids_ref[r, p, receiver * heads_dev + h] - first
                    slot_s[used] = slot
                    held = jnp.logical_and(slot >= 0, slot < pool_slots)
                    used = used + held.astype(jnp.int32)
        for place in range(PER_PEER):
            slot = jnp.clip(slot_s[place], 0, pool_slots - 1)
            out_ref[receiver, place * state_rows : (place + 1) * state_rows, :] = state_ref[slot]
            for lag in range(lag_rows):
                row = 8 * place + lag
                lag_s[receiver, row : row + 1, :] = conv_s[lag, pl.ds(slot, 1), :]
        return 0

    lax.fori_loop(0, receivers, one_receiver, 0)
    out_ref[:, PER_PEER * state_rows :, :] = lag_s[...].astype(out_ref.dtype)


def column_tiles(width, body):
    tile = min(512, width)

    def one_tile(index, _):
        body(pl.ds(pl.multiple_of(index * tile, tile), tile))
        return 0

    lax.fori_loop(0, width // tile, one_tile, 0)


def from_hbm(array):
    return pltpu.with_memory_space_constraint(array, pltpu.HBM)


def load_kernel(*refs):
    count = (len(refs) - 1) // 2
    sems = refs[-1]
    copies = [
        pltpu.make_async_copy(refs[at], refs[count + at], sems.at[at]) for at in range(count)
    ]
    for copy in copies:
        copy.start()
    for copy in copies:
        copy.wait()


def load(*arrays):
    return pl.pallas_call(
        load_kernel,
        out_shape=[jax.ShapeDtypeStruct(a.shape, a.dtype) for a in arrays],
        in_specs=[pl.BlockSpec(memory_space=pltpu.HBM)] * len(arrays),
        out_specs=[pl.BlockSpec(memory_space=pltpu.VMEM)] * len(arrays),
        scratch_shapes=[pltpu.SemaphoreType.DMA((len(arrays),))],
        compiler_params=pltpu.CompilerParams(vmem_limit_bytes=VMEM_LIMIT),
        cost_estimate=pl.CostEstimate(flops=0, bytes_accessed=8 << 20, transcendentals=0),
        name="load",
    )(*[from_hbm(a) for a in arrays])


def stage_kernel(count, *refs):
    block_refs = refs[:count]
    weight_ref, rate_weight_ref, out_ref, joined_s = refs[count:]
    rows = block_refs[0].shape[0]
    width = weight_ref.shape[1]
    for at, block_ref in enumerate(block_refs):
        joined_s[at * rows : (at + 1) * rows, :] = block_ref[...]
    rates = rate_weight_ref.shape[0]
    out_ref[:, width:] = jnp.zeros((out_ref.shape[0], out_ref.shape[1] - width), jnp.float32)
    out_ref[:, width : width + rates] = lax.dot_general(
        joined_s[...],
        rate_weight_ref[...],
        (((1,), (1,)), ((), ())),
        preferred_element_type=jnp.float32,
    )

    def body(columns):
        out_ref[:, columns] = jnp.dot(
            joined_s[...], weight_ref[:, columns], preferred_element_type=jnp.float32
        )

    column_tiles(width, body)


def stage(blocks, weight, rate_weight):
    rows, depth = blocks[0].shape
    total = rows * len(blocks)
    width = weight.shape[1] + 128
    return kernel_call(
        functools.partial(stage_kernel, len(blocks)),
        jax.ShapeDtypeStruct((total, width), jnp.float32),
        [*blocks, weight, rate_weight],
        [pltpu.VMEM((total, depth), jnp.bfloat16)],
        "stage",
        flops=2 * 256 * depth * width,
    )


def early_kernel(count, tile, *refs):
    block_refs = refs[:count]
    weight_ref, rate_weight_ref, out_hbm, held_s, joined_s, out_ref, sems = refs[count:]
    rows = block_refs[0].shape[0]
    width = weight_ref.shape[1]
    lefts = range(0, width, tile)
    loads = [
        pltpu.make_async_copy(
            weight_ref.at[:, pl.ds(left, tile)], held_s.at[:, pl.ds(left, tile)], sems.at[at]
        )
        for at, left in enumerate(lefts)
    ]
    for copy in loads:
        copy.start()
    for at, block_ref in enumerate(block_refs):
        joined_s[at * rows : (at + 1) * rows, :] = block_ref[...]
    rates = rate_weight_ref.shape[0]
    out_ref[:, width:] = jnp.zeros((out_ref.shape[0], out_ref.shape[1] - width), jnp.float32)
    out_ref[:, width : width + rates] = lax.dot_general(
        joined_s[...],
        rate_weight_ref[...],
        (((1,), (1,)), ((), ())),
        preferred_element_type=jnp.float32,
    )
    for left, copy in zip(lefts, loads, strict=True):
        copy.wait()
        out_ref[:, left : left + tile] = jnp.dot(
            joined_s[...], held_s[:, left : left + tile], preferred_element_type=jnp.float32
        )
    store = pltpu.make_async_copy(out_ref, out_hbm, sems.at[len(loads)])
    store.start()
    store.wait()


def early_stage(blocks, weight, rate_weight):
    rows, depth = blocks[0].shape
    count = len(blocks)
    width = weight.shape[1]
    tile = min(256, width)
    whole = pl.BlockSpec(memory_space=pltpu.VMEM)
    hbm = pl.BlockSpec(memory_space=pltpu.HBM)
    return pl.pallas_call(
        functools.partial(early_kernel, count, tile),
        out_shape=jax.ShapeDtypeStruct((rows * count, width + 128), jnp.float32),
        in_specs=[whole] * count + [hbm, whole],
        out_specs=hbm,
        scratch_shapes=[
            pltpu.VMEM((depth, width), jnp.bfloat16),
            pltpu.VMEM((rows * count, depth), jnp.bfloat16),
            pltpu.VMEM((rows * count, width + 128), jnp.float32),
            pltpu.SemaphoreType.DMA((width // tile + 1,)),
        ],
        compiler_params=pltpu.CompilerParams(vmem_limit_bytes=VMEM_LIMIT),
        cost_estimate=pl.CostEstimate(
            flops=2 * 256 * depth * width, bytes_accessed=8 << 20, transcendentals=0
        ),
        name="early_stage",
    )(*blocks, from_hbm(weight), rate_weight)


def part_kernel(mine_ref, weight_ref, out_ref):
    def body(columns):
        out_ref[:, columns] = jnp.dot(
            mine_ref[...], weight_ref[:, columns], preferred_element_type=jnp.float32
        )

    column_tiles(out_ref.shape[1], body)


def first_kernel(rows, part_ref, theirs_ref, held_ref, first_ref, second_ref):
    def body(columns):
        total = part_ref[: 2 * rows, columns] + jnp.dot(
            theirs_ref[: 2 * rows, :], held_ref[:, columns], preferred_element_type=jnp.float32
        )
        first_ref[:, columns] = total[:rows].astype(first_ref.dtype)
        second_ref[:, columns] = total[rows:].astype(second_ref.dtype)

    column_tiles(held_ref.shape[1], body)


def rest_kernel(rows, part_ref, theirs_ref, held_ref, out_ref):
    def body(columns):
        out_ref[:, columns] = part_ref[2 * rows :, columns] + jnp.dot(
            theirs_ref[2 * rows :, :], held_ref[:, columns], preferred_element_type=jnp.float32
        )

    column_tiles(held_ref.shape[1], body)


def add_kernel(top, share_ref, *refs):
    out_ref = refs[-1]
    total = share_ref[top : top + out_ref.shape[0], :]
    for arrived_ref in refs[:-1]:
        total = total + arrived_ref[...].astype(jnp.float32)
    out_ref[...] = total.astype(out_ref.dtype)


def gather_slots(half):
    slots = [(0, 0), (0, 1)]
    for step in range(1, half):
        slots += [(-step, 0), (-step, 1), (step, 1), (step, 0)]
    return slots + [(-half, 0), (half, 1)]


def send_slots(half):
    slots = []
    for step in range(half, 0, -1):
        slots.append((step, 0))
        if step > 1:
            slots.append((step - 1, 1))
    return slots + [(0, 0)]


def mix_kernel(sizes, scalar_ref, page_id_ref, number_ref, page_ref, *rest):
    heads_dev, piece_count, pool_slots, stages = sizes
    taps_ref, conv_bias_ref, gain_ref = rest[:3]
    stage_refs, rest = rest[3 : 3 + stages], rest[3 + stages :]
    conv_bias = conv_bias_ref[...].astype(jnp.float32).reshape(1, -1)
    gains = gain_ref[...].astype(jnp.float32).reshape(1, -1)
    state_ref, conv_ref, mine_ref, theirs_ref = rest[:4]
    placed_s, rows_s, rate_s, input_s, normed_s, initial_s, page_s, inverse_s, used_s = rest[4:]
    blocks, rows_dev, _ = placed_s.shape
    live_rows = SPAN - BLK
    lead = 8
    state_rows = HEAD_DIM // piece_count
    channels = HEAD_DIM + 2 * STATE
    row_width = HEAD_DIM + channels
    piece_channels = channels // piece_count
    blocks_req = blocks // REQS

    chip_count = blocks // 2
    half = chip_count // 2
    my_index = scalar_ref[0]
    core = my_index % 2
    place = place_of(my_index // 2, chip_count)
    owner_at = 1 + REQS

    def device_at(distance, flip):
        onto = place + jnp.where(core == 0, distance, -distance) + chip_count
        chip = chip_at(lax.rem(onto, chip_count), chip_count)
        return 2 * chip + (core if flip == 0 else 1 - core)

    def clear(holder, _):
        used_s[holder] = 0
        return 0

    lax.fori_loop(0, blocks, clear, 0)

    def invert(block, _):
        inverse_s[scalar_ref[owner_at + block]] = block
        return 0

    lax.fori_loop(0, blocks, invert, 0)

    page_s[...] = page_ref[...].astype(jnp.float32)

    pieces_of = []
    for r in range(REQS):
        for j in range(blocks_req):
            start = j * rows_dev
            low, high = max(start, BLK), start + rows_dev
            if high > BLK:
                pieces_of.append((r, r * blocks_req + j, low - start, low - BLK, high - BLK))
    slots = gather_slots(half)
    at = 0
    for stage_ref in stage_refs:
        for top in range(0, stage_ref.shape[0], rows_dev):
            placed_s[device_at(*slots[at])] = stage_ref[top : top + rows_dev, :]
            at += 1
    for r, block, skipped, low, high in pieces_of:
        rows_s[r, lead + low : lead + high, :] = placed_s[block, skipped:, : rows_s.shape[2]]
        rate_s[r, low:high, :] = placed_s[block, skipped:, rows_s.shape[2] :]
    normed_s[...] = jnp.zeros_like(normed_s)

    wide = (live_rows, 128)
    later = lax.broadcasted_iota(jnp.int32, (live_rows, live_rows), 0)
    sooner = lax.broadcasted_iota(jnp.int32, (live_rows, live_rows), 1)
    causal = later >= sooner
    ones = causal.astype(jnp.float32)
    position = lax.broadcasted_iota(jnp.int32, wide, 0) + BLK
    lead_position = lax.broadcasted_iota(jnp.int32, (live_rows + lead, channels), 0) + BLK - lead
    spread_row = lax.broadcasted_iota(jnp.int32, (piece_count * 128, channels), 0)
    spread_col = lax.broadcasted_iota(jnp.int32, (piece_count * 128, channels), 1)
    spread = (
        ((spread_row // 128) * piece_channels + spread_row % 128 == spread_col)
        & (spread_row % 128 < piece_channels)
    ).astype(jnp.bfloat16)

    lane = lax.broadcasted_iota(jnp.int32, (1, 128), 1)
    bias_lanes = jnp.zeros((1, 128), jnp.float32)
    decay_lanes = jnp.zeros((1, 128), jnp.float32)
    for h in range(heads_dev):
        bias_lanes = jnp.where(lane == h, number_ref[h], bias_lanes)
        decay_lanes = jnp.where(lane == h, number_ref[heads_dev + h], decay_lanes)

    for r in range(REQS):
        live_start = scalar_ref[1 + r] * BLK
        live = position >= live_start
        rate = rate_s[r] + bias_lanes
        step = jnp.where(live, jax.nn.softplus(rate), 0.0)
        drop = -decay_lanes * step
        total = jnp.dot(
            ones, drop, preferred_element_type=jnp.float32, precision=lax.Precision.HIGHEST
        )
        total_t = total.T
        step_t = step.T
        from_start = jnp.exp(total)
        span_tail = total[live_rows - 1 : live_rows, :]
        to_end = jnp.exp(span_tail - total) * step
        kept = jnp.exp(span_tail)
        for h in range(heads_dev):
            lags = []
            for p in range(piece_count):
                page = page_id_ref[r, p, my_index * heads_dev + h]
                holder = lax.div(page, pool_slots)
                rank = used_s[holder]
                used_s[holder] = rank + 1
                state_at = pl.ds(pl.multiple_of(rank * state_rows, state_rows), state_rows)
                lag_at = pl.ds(pl.multiple_of(PER_PEER * state_rows + 8 * rank, 8), 8)
                initial_s[p * state_rows : (p + 1) * state_rows, :] = page_s[holder, state_at, :]
                lags.append(page_s[holder, lag_at, :].astype(jnp.bfloat16))
            initial = initial_s[...]
            lag_lanes = jnp.concatenate(lags, axis=1)
            cached = jnp.dot(lag_lanes, spread, preferred_element_type=jnp.float32)
            first = h * row_width
            c0 = h * channels
            raw = rows_s[r, :, first + HEAD_DIM : first + row_width]
            raw = raw.astype(jnp.bfloat16).astype(jnp.float32)
            inputs = jnp.where(lead_position >= live_start, raw, 0.0)
            for lag in range(CONV - 1):
                inputs = jnp.where(
                    lead_position == live_start - (CONV - 1) + lag,
                    cached[lag : lag + 1, :],
                    inputs,
                )
            input_s[...] = inputs
            conv_ref[r, :, c0 : c0 + channels] = rows_s[
                r,
                live_rows + lead - (CONV - 1) : live_rows + lead,
                first + HEAD_DIM : first + row_width,
            ].astype(jnp.bfloat16)
            summed = jnp.broadcast_to(
                conv_bias[:, c0 : c0 + channels], (live_rows, channels)
            )
            for tap in range(CONV):
                begin = lead - (CONV - 1) + tap
                summed = summed + taps_ref[tap : tap + 1, c0 : c0 + channels].astype(
                    jnp.float32
                ) * input_s[begin : begin + live_rows, :]
            mixed_in = (summed * jax.nn.sigmoid(summed)).astype(jnp.bfloat16)
            x_part = mixed_in[:, :HEAD_DIM]
            b_part = mixed_in[:, HEAD_DIM : HEAD_DIM + STATE]
            c_part = mixed_in[:, HEAD_DIM + STATE :]
            x_float = x_part.astype(jnp.float32)
            last = (((1,), (1,)), ((), ()))
            scores = lax.dot_general(c_part, b_part, last, preferred_element_type=jnp.float32)
            gaps = jnp.where(causal, total[:, h : h + 1] - total_t[h : h + 1, :], 0.0)
            weights = jnp.where(causal, jnp.exp(gaps) * scores * step_t[h : h + 1, :], 0.0)
            outputs = jnp.dot(
                weights.astype(jnp.bfloat16), x_part, preferred_element_type=jnp.float32
            )
            reader = (c_part.astype(jnp.float32) * from_start[:, h : h + 1]).astype(jnp.bfloat16)
            outputs = outputs + lax.dot_general(
                reader, initial.astype(jnp.bfloat16), last, preferred_element_type=jnp.float32
            )
            outputs = outputs + number_ref[2 * heads_dev + h] * x_float
            entering = (x_float * to_end[:, h : h + 1]).astype(jnp.bfloat16)
            added = lax.dot_general(
                entering,
                b_part,
                (((0,), (0,)), ((), ())),
                preferred_element_type=jnp.float32,
            )
            state_ref[r, h] = kept[:, h : h + 1] * initial + added
            gate = rows_s[r, lead:, first : first + HEAD_DIM]
            gate = gate.astype(jnp.bfloat16).astype(jnp.float32)
            gated = outputs * (gate * jax.nn.sigmoid(gate))
            scale = lax.rsqrt(jnp.mean(gated * gated, axis=1, keepdims=True) + EPSILON)
            gain = gains[:, h * HEAD_DIM : (h + 1) * HEAD_DIM]
            normed = jnp.where(live, gated * scale * gain, 0.0)
            for rr, block, skipped, low, high in pieces_of:
                if rr == r:
                    normed_s[block, skipped:, h * HEAD_DIM : (h + 1) * HEAD_DIM] = normed[low:high]

    for at, (distance, flip) in enumerate(send_slots(half)):
        rows = slice(at * rows_dev, (at + 1) * rows_dev)
        mine_ref[rows, :] = normed_s[inverse_s[device_at(distance, flip)]].astype(jnp.bfloat16)
        theirs_ref[rows, :] = normed_s[inverse_s[device_at(-distance, 1 - flip)]].astype(
            jnp.bfloat16
        )


def body(
    hidden,
    in_weight,
    dt_weight,
    dt_bias,
    decay_rate,
    conv_weight,
    conv_bias,
    skip,
    norm_gain,
    out_weight,
    state_pool,
    conv_pool,
    hit_page,
    prefix_blocks,
    owners,
):
    device_count = lax.axis_size("dp")
    my_index = lax.axis_index("dp").astype(jnp.int32).reshape(1)
    heads_dev = dt_weight.shape[0]
    piece_count = hit_page.shape[2]
    row_width = 2 * HEAD_DIM + 2 * STATE
    channels = HEAD_DIM + 2 * STATE
    rows_dev = hidden.shape[0]
    pool_slots, state_rows, _ = state_pool.shape
    chip_count = device_count // 2
    half = chip_count // 2
    page_ids = jnp.swapaxes(hit_page, 1, 2)

    other_type = other_core(hidden, chip_count)
    page_rows = PER_PEER * state_rows + 8 * PER_PEER
    entries = REQS * heads_dev * piece_count
    offered = kernel_call(
        functools.partial(offer_kernel, entries),
        jax.ShapeDtypeStruct((device_count, page_rows, STATE), state_pool.dtype),
        [
            my_index,
            page_ids,
            from_hbm(state_pool),
            from_hbm(jnp.swapaxes(conv_pool, 0, 1)),
        ],
        [
            pltpu.SMEM((entries + 1,), jnp.int32),
            pltpu.VMEM((CONV - 1, pool_slots, STATE), jnp.float32),
            pltpu.VMEM((device_count, 8 * PER_PEER, STATE), jnp.float32),
        ],
        "offer_pages",
        smem=2,
        limit=VMEM_ALL,
    )
    own_type = stream(hidden, chip_count)
    first_other = other_type
    other_type = stream_other(hidden, chip_count)
    scalars = jnp.concatenate([my_index, prefix_blocks, owners])
    numbers = jnp.concatenate([dt_bias, decay_rate, skip])
    offered, own_type, other_type, scalars, numbers, held = lax.optimization_barrier(
        (offered, own_type, other_type, scalars, numbers, out_weight)
    )
    received = lax.all_to_all(offered, "dp", split_axis=0, concat_axis=0, tiled=True)
    held = other_core(held, chip_count)
    blocks = [from_hbm(hidden), first_other, own_type, other_type]
    blocks += [other_core(own_type, chip_count), other_core(other_type, chip_count)]
    early = early_stage(blocks, in_weight, from_hbm(dt_weight))
    pending = []
    for step in range(2, half):
        own_type = stream(own_type, chip_count)
        other_type = stream(other_type, chip_count)
        if step == 2:
            own_type, early = lax.optimization_barrier((own_type, early))
            staged = [from_hbm(early)]
            received, weight_here, rates_here = lax.optimization_barrier(
                (received, in_weight, dt_weight)
            )
            weight_here, rates_here = load(weight_here, rates_here)
        if step == half - 1:
            own_type, weight_here = lax.optimization_barrier((own_type, weight_here))
        pending += [
            own_type,
            other_type,
            other_core(own_type, chip_count),
            other_core(other_type, chip_count),
        ]
        if len(pending) >= 6 or step == half - 1:
            staged.append(stage(pending, weight_here, rates_here))
            pending = []
    own_type = stream(own_type, chip_count)
    last = [own_type, other_core(own_type, chip_count)]
    staged.append(stage(last, weight_here, rates_here))

    live_rows = SPAN - BLK
    normed_rows = jax.ShapeDtypeStruct((chip_count * rows_dev, heads_dev * HEAD_DIM), jnp.bfloat16)
    final_state, final_conv, mine, theirs = kernel_call(
        functools.partial(mix_kernel, (heads_dev, piece_count, pool_slots, len(staged))),
        [
            jax.ShapeDtypeStruct((REQS, heads_dev, HEAD_DIM, STATE), jnp.float32),
            jax.ShapeDtypeStruct((REQS, CONV - 1, heads_dev * channels), jnp.bfloat16),
            normed_rows,
            normed_rows,
        ],
        [
            scalars,
            page_ids,
            numbers,
            received,
            conv_weight,
            conv_bias,
            norm_gain,
            *staged,
        ],
        [
            pltpu.VMEM((device_count, rows_dev, heads_dev * row_width + 128), jnp.float32),
            pltpu.VMEM((REQS, live_rows + 8, heads_dev * row_width), jnp.float32),
            pltpu.VMEM((REQS, live_rows, 128), jnp.float32),
            pltpu.VMEM((live_rows + 8, channels), jnp.float32),
            pltpu.VMEM((device_count, rows_dev, heads_dev * HEAD_DIM), jnp.float32),
            pltpu.VMEM((HEAD_DIM, STATE), jnp.float32),
            pltpu.VMEM(received.shape, jnp.float32),
            pltpu.SMEM((device_count,), jnp.int32),
            pltpu.SMEM((device_count,), jnp.int32),
        ],
        "mixer",
        flops=1 << 30,
        smem=3,
    )

    theirs = other_core(theirs, chip_count)
    width = out_weight.shape[1]
    total_rows = chip_count * rows_dev
    block = jax.ShapeDtypeStruct((rows_dev, width), jnp.bfloat16)
    part = kernel_call(
        part_kernel,
        jax.ShapeDtypeStruct((total_rows, width), jnp.float32),
        [mine, out_weight],
        [],
        "sums_part",
        flops=1 << 30,
    )
    first, second = kernel_call(
        functools.partial(first_kernel, rows_dev),
        [block, block],
        [part, theirs, held],
        [],
        "sums_first",
        flops=1 << 30,
    )
    own_sum = stream(first, chip_count)
    other_sum = stream(second, chip_count)
    shares = kernel_call(
        functools.partial(rest_kernel, rows_dev),
        jax.ShapeDtypeStruct((total_rows - 2 * rows_dev, width), jnp.float32),
        [part, theirs, held],
        [],
        "sums_rest",
        flops=1 << 30,
    )

    def onward(at, *arrived):
        top = (at - 2) * rows_dev
        return kernel_call(
            functools.partial(add_kernel, top), block, [shares, *arrived], [], "onward"
        )

    slots = send_slots(half)
    for at in range(2, len(slots) - 1):
        if slots[at][1] == 0:
            own_sum = stream(onward(at, own_sum), chip_count)
        else:
            other_sum = stream(onward(at, other_sum), chip_count)
    crossed = other_core(other_sum, chip_count)
    mixed = onward(len(slots) - 1, own_sum, crossed)
    return (mixed, final_state, final_conv)


def solution(mesh):
    return jax.shard_map(
        body,
        mesh=mesh,
        in_specs=(
            P(("groups", "dp"), None),
            P(None, "dp"),
            P("dp", None),
            P("dp"),
            P("dp"),
            P(None, "dp"),
            P("dp"),
            P("dp"),
            P("dp"),
            P("dp", None),
            P(("groups", "dp"), None, None),
            P(("groups", "dp"), None, None),
            P("groups", None, None),
            P("groups"),
            P("groups"),
        ),
        out_specs=(
            P(("groups", "dp"), None),
            P("groups", "dp", None, None),
            P("groups", None, "dp"),
        ),
        check_vma=False,
    )
```

profile of v0, /device:TPU:0, one launch (start us, length us, event | category | flops | bytes accessed | tf_op | source)
XLA Modules:
  0.0 77.5 jit_solution(17887381754609940744)
XLA Ops:
  0.6 3.1 %collective-permute-start = (bf16[24,4096]{1,0:T(8,128)(2,1)}, bf16[24,4096]{1,0:T(8,128)(2,1)S(1)}, u32[]{:S(2)}, u32[]{:S(2)}) collective-permute-start(bf16[24,4096]{1,0:T(8,128)(2,1)} %refs_0_.1), channel_id=1, source_target_pairs={{0,4},{1,3},{4,8},{5,1},{8,12},{9,5},{12,14},{13,9},{14,10},{15,13... | collective-permute-start | bytes 589832 | tf_op jit(solution)/shard_map/ppermute | solution.py:49
  3.7 0.7 collective-permute-start.1
  4.4 2.7 %offer_pages.1 = bf16[16,80,128]{2,1,0:T(8,128)(2,1)} custom-call(s32[1]{0:T(128)} %bitcast.my_ref, s32[2,4,32]{2,1,0:T(4,128)} %bitcast.3, bf16[32,32,128]{2,1,0:T(8,128)(2,1)} %state_ref.1, bf16[3,32,96]{2,1,0:T(8,128)(2,1)} %bitcast.5), custom_call_target="tpu_custom_call" | custom-call | bytes 8388608 | tf_op jit(solution)/shard_map/offer_pages/pallas_call | solution.py:71
  7.1 0.7 pad_add_fusion.scalar_ref
  7.9 0.8 pad_maximum_fusion.number_ref
  8.6 0.0 collective-permute-done.refs_2_
  8.7 1.0 %collective-permute-done.1.refs_3_ = bf16[24,4096]{1,0:T(8,128)(2,1)S(1)} collective-permute-done((bf16[24,4096]{1,0:T(8,128)(2,1)}, bf16[24,4096]{1,0:T(8,128)(2,1)S(1)}, u32[]{:S(2)}, u32[]{:S(2)}) %collective-permute-start.1) | collective-permute-done | bytes 196640 | tf_op jit(solution)/shard_map/ppermute | solution.py:60
  9.6 0.1 collective-permute-start.16
  9.7 6.3 %all-to-all-start = ((bf16[16,80,128]{2,1,0:T(8,128)(2,1)}), bf16[16,80,128]{2,1,0:T(8,128)(2,1)S(1)}, u32[]{:S(2)}, u32[]{:S(2)}) async-start(bf16[16,80,128]{2,1,0:T(8,128)(2,1)} %offer_pages.1), calls=%async_computation | async-start | bytes 655360 | tf_op jit(solution)/shard_map/all_to_all | solution.py:542
  16.1 0.4 collective-permute-start.3
  16.5 0.2 collective-permute-start.4
  16.6 0.3 collective-permute-start.5
  17.0 1.7 %collective-permute-start.2 = (bf16[24,4096]{1,0:T(8,128)(2,1)S(1)}, bf16[24,4096]{1,0:T(8,128)(2,1)S(1)}, u32[]{:S(2)}, u32[]{:S(2)}) collective-permute-start(bf16[24,4096]{1,0:T(8,128)(2,1)S(1)} %collective-permute-done.refs_2_), channel_id=1, source_target_pairs={{0,4},{1,3},{4,8},{5,1},{8,12},{9,5},{12,14},{13,9},{14,10},{15,13... | collective-permute-start | bytes 589832 | tf_op jit(solution)/shard_map/ppermute | solution.py:49
  18.6 0.0 collective-permute-done.3.refs_1_
  18.6 1.5 %collective-permute-start.6 = (bf16[24,4096]{1,0:T(8,128)(2,1)S(1)}, bf16[24,4096]{1,0:T(8,128)(2,1)S(1)}, u32[]{:S(2)}, u32[]{:S(2)}) collective-permute-start(bf16[24,4096]{1,0:T(8,128)(2,1)S(1)} %collective-permute-done.1.refs_3_), channel_id=1, source_target_pairs={{0,4},{1,3},{4,8},{5,1},{8,12},{9,5},{12,14},{13,9},{14,10},{15,13... | collective-permute-start | bytes 589832 | tf_op jit(solution)/shard_map/ppermute | solution.py:49
  20.1 0.0 collective-permute-done.4.refs_4_
  20.1 0.0 collective-permute-done.5.refs_5_
  20.1 6.1 %early_stage.1.rest_3_ = f32[144,1152]{1,0:T(8,128)S(1)} custom-call(bf16[24,4096]{1,0:T(8,128)(2,1)} %refs_0_.1, bf16[24,4096]{1,0:T(8,128)(2,1)S(1)} %collective-permute-done.3.refs_1_, bf16[24,4096]{1,0:T(8,128)(2,1)S(1)} %collective-permute-done.refs_2_, bf16[24,4096]{1,0:T(8,128)(2,1)S(1)} %collective-permute-done.1.refs_3_, ...), custom_call_target="tpu_custom_call" | custom-call | flops 2147483648 | bytes 8388608 | tf_op jit(solution)/shard_map/early_stage/pallas_call | solution.py:233
  26.3 0.8 %copy-done.1 = f32[144,1152]{1,0:T(8,128)} copy-done((f32[144,1152]{1,0:T(8,128)}, f32[144,1152]{1,0:T(8,128)S(1)}, u32[]{:S(2)}) %copy-start.1) | copy-done | bytes 663576
  27.1 0.0 collective-permute-done.2.refs_0_
  27.1 1.5 %collective-permute-start.9 = (bf16[24,4096]{1,0:T(8,128)(2,1)S(1)}, bf16[24,4096]{1,0:T(8,128)(2,1)S(1)}, u32[]{:S(2)}, u32[]{:S(2)}) collective-permute-start(bf16[24,4096]{1,0:T(8,128)(2,1)S(1)} %collective-permute-done.2.refs_0_), channel_id=1, source_target_pairs={{0,4},{1,3},{4,8},{5,1},{8,12},{9,5},{12,14},{13,9},{14,10},{15,13... | collective-permute-start | bytes 589832 | tf_op jit(solution)/shard_map/ppermute | solution.py:49
  28.6 0.0 collective-permute-done.6.refs_1_
  28.6 1.8 %collective-permute-start.10 = (bf16[24,4096]{1,0:T(8,128)(2,1)S(1)}, bf16[24,4096]{1,0:T(8,128)(2,1)S(1)}, u32[]{:S(2)}, u32[]{:S(2)}) collective-permute-start(bf16[24,4096]{1,0:T(8,128)(2,1)S(1)} %collective-permute-done.6.refs_1_), channel_id=1, source_target_pairs={{0,4},{1,3},{4,8},{5,1},{8,12},{9,5},{12,14},{13,9},{14,10},{15,13... | collective-permute-start | bytes 589832 | tf_op jit(solution)/shard_map/ppermute | solution.py:49
  30.3 0.5 collective-permute-start.8
  30.9 0.0 all-to-all-done.page_ref
  30.9 3.4 %load.1 = (bf16[4096,1024]{1,0:T(8,128)(2,1)S(1)}, bf16[2,4096]{1,0:T(2,128)(2,1)S(1)}) custom-call(bf16[4096,1024]{1,0:T(8,128)(2,1)} %refs_0_.2, bf16[2,4096]{1,0:T(2,128)(2,1)} %refs_1_), custom_call_target="tpu_custom_call" | custom-call | bytes 8388608 | tf_op jit(solution)/shard_map/load/pallas_call | solution.py:142
  34.3 0.0 collective-permute-done.9.refs_4_
  34.3 2.2 %collective-permute-start.13 = (bf16[24,4096]{1,0:T(8,128)(2,1)S(1)}, bf16[24,4096]{1,0:T(8,128)(2,1)S(1)}, u32[]{:S(2)}, u32[]{:S(2)}) collective-permute-start(bf16[24,4096]{1,0:T(8,128)(2,1)S(1)} %collective-permute-done.9.refs_4_), channel_id=1, source_target_pairs={{0,4},{1,3},{4,8},{5,1},{8,12},{9,5},{12,14},{13,9},{14,10},{15,13... | collective-permute-start | bytes 589832 | tf_op jit(solution)/shard_map/ppermute | solution.py:49
  36.4 0.0 collective-permute-start.12
  36.4 0.0 collective-permute-done.7.refs_2_
  36.4 0.5 collective-permute-start.11
  37.0 3.0 %collective-permute-done.13.refs_0_ = bf16[24,4096]{1,0:T(8,128)(2,1)S(1)} collective-permute-done((bf16[24,4096]{1,0:T(8,128)(2,1)S(1)}, bf16[24,4096]{1,0:T(8,128)(2,1)S(1)}, u32[]{:S(2)}, u32[]{:S(2)}) %collective-permute-start.13) | collective-permute-done | bytes 196640 | tf_op jit(solution)/shard_map/ppermute | solution.py:49
  40.0 0.0 collective-permute-start.14
  40.0 3.5 %stage.2.rest_4_ = f32[192,1152]{1,0:T(8,128)S(1)} custom-call(bf16[24,4096]{1,0:T(8,128)(2,1)S(1)} %collective-permute-done.2.refs_0_, bf16[24,4096]{1,0:T(8,128)(2,1)S(1)} %collective-permute-done.6.refs_1_, bf16[24,4096]{1,0:T(8,128)(2,1)S(1)} %collective-permute-done.7.refs_2_, bf16[24,4096]{1,0:T(8,128)(2,1)} %collective-permute-done.8.refs_3_, ...), custom_call_target="tpu_custom_call" | custom-call | flops 2415919104 | bytes 8388608 | tf_op jit(solution)/shard_map/stage/pallas_call | solution.py:71
  43.5 0.0 copy-start.2
  43.5 0.0 copy-start.3
  43.5 0.0 copy-start.4
  43.6 0.0 copy-start.5
  43.6 1.9 %stage.3.rest_5_ = f32[48,1152]{1,0:T(8,128)S(1)} custom-call(bf16[24,4096]{1,0:T(8,128)(2,1)S(1)} %collective-permute-done.13.refs_0_, bf16[24,4096]{1,0:T(8,128)(2,1)S(1)} %collective-permute-done.14.refs_1_, bf16[4096,1024]{1,0:T(8,128)(2,1)S(1)} %get-tuple-element.36.refs_8_.refs_2_, bf16[2,4096]{1,0:T(2,128)(2,1)S(1)} %get-tuple-element.37.refs_9_.refs_3_), custom_call_target="tpu_custom_call" | custom-call | flops 2415919104 | bytes 8388608 | tf_op jit(solution)/shard_map/stage/pallas_call | solution.py:71
  45.5 0.0 copy-done.2
  45.6 0.0 copy-start
  45.6 4.6 %mixer.1 = (f32[2,2,128,128]{3,2,1,0:T(8,128)}, bf16[2,3,768]{2,1,0:T(4,128)(2,1)S(1)}, bf16[192,256]{1,0:T(8,128)(2,1)S(1)}, bf16[192,256]{1,0:T(8,128)(2,1)S(1)}) custom-call(s32[19]{0:T(128)S(1)} %pad_add_fusion.scalar_ref, s32[2,4,32]{2,1,0:T(4,128)S(1)} %bitcast.4, f32[6]{0:T(128)S(1)} %pad_maximum_fusion.number_ref, ...), custom_call_target="tpu_custom_call" | custom-call | flops 1073741824 | bytes 8388608 | tf_op jit(solution)/shard_map/mixer/pallas_call | solution.py:71
  50.2 0.5 collective-permute-start.15
  50.7 1.7 %sums_part.1.part_ref = f32[192,4096]{1,0:T(8,128)S(1)} custom-call(bf16[192,256]{1,0:T(8,128)(2,1)S(1)} %get-tuple-element.38.mine_ref, bf16[256,4096]{1,0:T(8,128)(2,1)S(1)} %copy-done), custom_call_target="tpu_custom_call" | custom-call | flops 1073741824 | bytes 8388608 | tf_op jit(solution)/shard_map/sums_part/pallas_call | solution.py:71
  52.4 1.3 %sums_first.1 = (bf16[24,4096]{1,0:T(8,128)(2,1)S(1)}, bf16[24,4096]{1,0:T(8,128)(2,1)S(1)}) custom-call(f32[192,4096]{1,0:T(8,128)S(1)} %sums_part.1.part_ref, bf16[192,256]{1,0:T(8,128)(2,1)S(1)} %collective-permute-done.15.theirs_ref, bf16[256,4096]{1,0:T(8,128)(2,1)S(1)} %collective-permute-done.16.held_ref), custom_call_target="tpu_custom_call" | custom-call | flops 1073741824 | bytes 8388608 | tf_op jit(solution)/shard_map/sums_first/pallas_call | solution.py:71
  53.7 2.1 %collective-permute-start.17 = (bf16[24,4096]{1,0:T(8,128)(2,1)S(1)}, bf16[24,4096]{1,0:T(8,128)(2,1)S(1)}, u32[]{:S(2)}, u32[]{:S(2)}) collective-permute-start(bf16[24,4096]{1,0:T(8,128)(2,1)S(1)} %get-tuple-element.41), channel_id=1, source_target_pairs={{0,4},{1,3},{4,8},{5,1},{8,12},{9,5},{12,14},{13,9},{14,10},{15,13... | collective-permute-start | bytes 589832 | tf_op jit(solution)/shard_map/ppermute | solution.py:49
  55.9 0.5 collective-permute-start.21
  56.4 1.6 %sums_rest.1.share_ref = f32[144,4096]{1,0:T(8,128)S(1)} custom-call(f32[192,4096]{1,0:T(8,128)S(1)} %sums_part.1.part_ref, bf16[192,256]{1,0:T(8,128)(2,1)S(1)} %collective-permute-done.15.theirs_ref, bf16[256,4096]{1,0:T(8,128)(2,1)S(1)} %collective-permute-done.16.held_ref), custom_call_target="tpu_custom_call" | custom-call | flops 1073741824 | bytes 8388608 | tf_op jit(solution)/shard_map/sums_rest/pallas_call | solution.py:71
  58.0 1.5 %collective-permute-done.17.refs_0_ = bf16[24,4096]{1,0:T(8,128)(2,1)S(1)} collective-permute-done((bf16[24,4096]{1,0:T(8,128)(2,1)S(1)}, bf16[24,4096]{1,0:T(8,128)(2,1)S(1)}, u32[]{:S(2)}, u32[]{:S(2)}) %collective-permute-start.17) | collective-permute-done | bytes 196640 | tf_op jit(solution)/shard_map/ppermute | solution.py:49
  59.5 2.1 %collective-permute-start.18 = (bf16[24,4096]{1,0:T(8,128)(2,1)S(1)}, bf16[24,4096]{1,0:T(8,128)(2,1)S(1)}, u32[]{:S(2)}, u32[]{:S(2)}) collective-permute-start(bf16[24,4096]{1,0:T(8,128)(2,1)S(1)} %onward.6), channel_id=1, source_target_pairs={{0,4},{1,3},{4,8},{5,1},{8,12},{9,5},{12,14},{13,9},{14,10},{15,13... | collective-permute-start | bytes 589832 | tf_op jit(solution)/shard_map/ppermute | solution.py:49
  61.6 0.0 collective-permute-done.21.refs_0_
  61.7 2.1 %collective-permute-start.22 = (bf16[24,4096]{1,0:T(8,128)(2,1)S(1)}, bf16[24,4096]{1,0:T(8,128)(2,1)S(1)}, u32[]{:S(2)}, u32[]{:S(2)}) collective-permute-start(bf16[24,4096]{1,0:T(8,128)(2,1)S(1)} %onward.9), channel_id=1, source_target_pairs={{0,4},{1,3},{4,8},{5,1},{8,12},{9,5},{12,14},{13,9},{14,10},{15,13... | collective-permute-start | bytes 589832 | tf_op jit(solution)/shard_map/ppermute | solution.py:49
  63.7 1.5 %collective-permute-done.18.refs_0_ = bf16[24,4096]{1,0:T(8,128)(2,1)S(1)} collective-permute-done((bf16[24,4096]{1,0:T(8,128)(2,1)S(1)}, bf16[24,4096]{1,0:T(8,128)(2,1)S(1)}, u32[]{:S(2)}, u32[]{:S(2)}) %collective-permute-start.18) | collective-permute-done | bytes 196640 | tf_op jit(solution)/shard_map/ppermute | solution.py:49
  65.3 2.1 %collective-permute-start.19 = (bf16[24,4096]{1,0:T(8,128)(2,1)S(1)}, bf16[24,4096]{1,0:T(8,128)(2,1)S(1)}, u32[]{:S(2)}, u32[]{:S(2)}) collective-permute-start(bf16[24,4096]{1,0:T(8,128)(2,1)S(1)} %onward.7), channel_id=1, source_target_pairs={{0,4},{1,3},{4,8},{5,1},{8,12},{9,5},{12,14},{13,9},{14,10},{15,13... | collective-permute-start | bytes 589832 | tf_op jit(solution)/shard_map/ppermute | solution.py:49
  67.4 0.0 collective-permute-done.22.refs_0_
  67.4 2.1 %collective-permute-start.23 = (bf16[24,4096]{1,0:T(8,128)(2,1)S(1)}, bf16[24,4096]{1,0:T(8,128)(2,1)S(1)}, u32[]{:S(2)}, u32[]{:S(2)}) collective-permute-start(bf16[24,4096]{1,0:T(8,128)(2,1)S(1)} %onward.10), channel_id=1, source_target_pairs={{0,4},{1,3},{4,8},{5,1},{8,12},{9,5},{12,14},{13,9},{14,10},{15,13... | collective-permute-start | bytes 589832 | tf_op jit(solution)/shard_map/ppermute | solution.py:49
  69.5 1.5 %collective-permute-done.19.refs_0_ = bf16[24,4096]{1,0:T(8,128)(2,1)S(1)} collective-permute-done((bf16[24,4096]{1,0:T(8,128)(2,1)S(1)}, bf16[24,4096]{1,0:T(8,128)(2,1)S(1)}, u32[]{:S(2)}, u32[]{:S(2)}) %collective-permute-start.19) | collective-permute-done | bytes 196640 | tf_op jit(solution)/shard_map/ppermute | solution.py:49
  71.0 2.1 %collective-permute-start.20 = (bf16[24,4096]{1,0:T(8,128)(2,1)S(1)}, bf16[24,4096]{1,0:T(8,128)(2,1)S(1)}, u32[]{:S(2)}, u32[]{:S(2)}) collective-permute-start(bf16[24,4096]{1,0:T(8,128)(2,1)S(1)} %onward.8), channel_id=1, source_target_pairs={{0,4},{1,3},{4,8},{5,1},{8,12},{9,5},{12,14},{13,9},{14,10},{15,13... | collective-permute-start | bytes 589832 | tf_op jit(solution)/shard_map/ppermute | solution.py:49
  73.2 0.0 collective-permute-done.23
  73.2 0.0 collective-permute-start.24
  73.2 0.6 copy.18
  73.8 3.0 %collective-permute-done.20.refs_0_ = bf16[24,4096]{1,0:T(8,128)(2,1)S(1)} collective-permute-done((bf16[24,4096]{1,0:T(8,128)(2,1)S(1)}, bf16[24,4096]{1,0:T(8,128)(2,1)S(1)}, u32[]{:S(2)}, u32[]{:S(2)}) %collective-permute-start.20) | collective-permute-done | bytes 196640 | tf_op jit(solution)/shard_map/ppermute | solution.py:49
  76.8 0.0 collective-permute-done.24.refs_1_
  76.8 0.7 onward.11
  (18 shorter events, 0.2 us)
Async XLA Ops:
  0.6 8.0 %collective-permute-start = (bf16[24,4096]{1,0:T(8,128)(2,1)}, bf16[24,4096]{1,0:T(8,128)(2,1)S(1)}, u32[]{:S(2)}, u32[]{:S(2)}) collective-permute-start(bf16[24,4096]{1,0:T(8,128)(2,1)} %refs_0_.1), channel_id=1, source_target_pairs={{0,4},{1,3},{4,8},{5,1},{8,12},{9,5},{12,14},{13,9},{14,10},{15,13... | collective-permute-start | bytes 589832 | tf_op jit(solution)/shard_map/ppermute | solution.py:49
  3.7 5.9 %collective-permute-start.1 = (bf16[24,4096]{1,0:T(8,128)(2,1)}, bf16[24,4096]{1,0:T(8,128)(2,1)S(1)}, u32[]{:S(2)}, u32[]{:S(2)}) collective-permute-start(bf16[24,4096]{1,0:T(8,128)(2,1)} %refs_0_.1), channel_id=1, source_target_pairs={{1,4},{0,3},{5,8},{4,1},{9,12},{8,5},{13,14},{12,9},{15,10},{14,13... | collective-permute-start | bytes 589832 | tf_op jit(solution)/shard_map/ppermute | solution.py:60
  9.6 42.8 %collective-permute-start.16 = (bf16[256,4096]{1,0:T(8,128)(2,1)}, bf16[256,4096]{1,0:T(8,128)(2,1)S(1)}, u32[]{:S(2)}, u32[]{:S(2)}) collective-permute-start(bf16[256,4096]{1,0:T(8,128)(2,1)} %weight_ref.1), channel_id=1, source_target_pairs={{0,1},{1,0},{2,3},{3,2},{4,5},{5,4},{6,7},{7,6},{8,9},{9,8},{10,11... | collective-permute-start | bytes 6291464 | tf_op jit(solution)/shard_map/ppermute | solution.py:64
  9.7 21.1 %all-to-all-start = ((bf16[16,80,128]{2,1,0:T(8,128)(2,1)}), bf16[16,80,128]{2,1,0:T(8,128)(2,1)S(1)}, u32[]{:S(2)}, u32[]{:S(2)}) async-start(bf16[16,80,128]{2,1,0:T(8,128)(2,1)} %offer_pages.1), calls=%async_computation | async-start | bytes 655360 | tf_op jit(solution)/shard_map/all_to_all | solution.py:542
  16.1 2.6 %collective-permute-start.3 = (bf16[24,4096]{1,0:T(8,128)(2,1)}, bf16[24,4096]{1,0:T(8,128)(2,1)S(1)}, u32[]{:S(2)}, u32[]{:S(2)}) collective-permute-start(bf16[24,4096]{1,0:T(8,128)(2,1)} %refs_0_.1), channel_id=1, source_target_pairs={{0,1},{1,0},{2,3},{3,2},{4,5},{5,4},{6,7},{7,6},{8,9},{9,8},{10,11... | collective-permute-start | bytes 589832 | tf_op jit(solution)/shard_map/ppermute | solution.py:64
  16.5 3.6 %collective-permute-start.4 = (bf16[24,4096]{1,0:T(8,128)(2,1)S(1)}, bf16[24,4096]{1,0:T(8,128)(2,1)S(1)}, u32[]{:S(2)}, u32[]{:S(2)}) collective-permute-start(bf16[24,4096]{1,0:T(8,128)(2,1)S(1)} %collective-permute-done.refs_2_), channel_id=1, source_target_pairs={{0,1},{1,0},{2,3},{3,2},{4,5},{5,4},{6,7},{7,6},{8,9},{9,8},{10,11... | collective-permute-start | bytes 589832 | tf_op jit(solution)/shard_map/ppermute | solution.py:64
  16.6 3.5 %collective-permute-start.5 = (bf16[24,4096]{1,0:T(8,128)(2,1)S(1)}, bf16[24,4096]{1,0:T(8,128)(2,1)S(1)}, u32[]{:S(2)}, u32[]{:S(2)}) collective-permute-start(bf16[24,4096]{1,0:T(8,128)(2,1)S(1)} %collective-permute-done.1.refs_3_), channel_id=1, source_target_pairs={{0,1},{1,0},{2,3},{3,2},{4,5},{5,4},{6,7},{7,6},{8,9},{9,8},{10,11... | collective-permute-start | bytes 589832 | tf_op jit(solution)/shard_map/ppermute | solution.py:64
  17.0 10.1 %collective-permute-start.2 = (bf16[24,4096]{1,0:T(8,128)(2,1)S(1)}, bf16[24,4096]{1,0:T(8,128)(2,1)S(1)}, u32[]{:S(2)}, u32[]{:S(2)}) collective-permute-start(bf16[24,4096]{1,0:T(8,128)(2,1)S(1)} %collective-permute-done.refs_2_), channel_id=1, source_target_pairs={{0,4},{1,3},{4,8},{5,1},{8,12},{9,5},{12,14},{13,9},{14,10},{15,13... | collective-permute-start | bytes 589832 | tf_op jit(solution)/shard_map/ppermute | solution.py:49
  18.6 9.9 %collective-permute-start.6 = (bf16[24,4096]{1,0:T(8,128)(2,1)S(1)}, bf16[24,4096]{1,0:T(8,128)(2,1)S(1)}, u32[]{:S(2)}, u32[]{:S(2)}) collective-permute-start(bf16[24,4096]{1,0:T(8,128)(2,1)S(1)} %collective-permute-done.1.refs_3_), channel_id=1, source_target_pairs={{0,4},{1,3},{4,8},{5,1},{8,12},{9,5},{12,14},{13,9},{14,10},{15,13... | collective-permute-start | bytes 589832 | tf_op jit(solution)/shard_map/ppermute | solution.py:49
  26.3 0.9 %copy-start.1 = (f32[144,1152]{1,0:T(8,128)}, f32[144,1152]{1,0:T(8,128)S(1)}, u32[]{:S(2)}) copy-start(f32[144,1152]{1,0:T(8,128)S(1)} %early_stage.1.rest_3_) | copy-start | bytes 1990660
  27.1 7.2 %collective-permute-start.9 = (bf16[24,4096]{1,0:T(8,128)(2,1)S(1)}, bf16[24,4096]{1,0:T(8,128)(2,1)S(1)}, u32[]{:S(2)}, u32[]{:S(2)}) collective-permute-start(bf16[24,4096]{1,0:T(8,128)(2,1)S(1)} %collective-permute-done.2.refs_0_), channel_id=1, source_target_pairs={{0,4},{1,3},{4,8},{5,1},{8,12},{9,5},{12,14},{13,9},{14,10},{15,13... | collective-permute-start | bytes 589832 | tf_op jit(solution)/shard_map/ppermute | solution.py:49
  28.6 7.9 %collective-permute-start.10 = (bf16[24,4096]{1,0:T(8,128)(2,1)S(1)}, bf16[24,4096]{1,0:T(8,128)(2,1)S(1)}, u32[]{:S(2)}, u32[]{:S(2)}) collective-permute-start(bf16[24,4096]{1,0:T(8,128)(2,1)S(1)} %collective-permute-done.6.refs_1_), channel_id=1, source_target_pairs={{0,4},{1,3},{4,8},{5,1},{8,12},{9,5},{12,14},{13,9},{14,10},{15,13... | collective-permute-start | bytes 589832 | tf_op jit(solution)/shard_map/ppermute | solution.py:49
  30.3 6.1 %collective-permute-start.7 = (bf16[24,4096]{1,0:T(8,128)(2,1)S(1)}, bf16[24,4096]{1,0:T(8,128)(2,1)S(1)}, u32[]{:S(2)}, u32[]{:S(2)}) collective-permute-start(bf16[24,4096]{1,0:T(8,128)(2,1)S(1)} %collective-permute-done.2.refs_0_), channel_id=1, source_target_pairs={{0,1},{1,0},{2,3},{3,2},{4,5},{5,4},{6,7},{7,6},{8,9},{9,8},{10,11... | collective-permute-start | bytes 589832 | tf_op jit(solution)/shard_map/ppermute | solution.py:64
  30.3 9.7 %collective-permute-start.8 = (bf16[24,4096]{1,0:T(8,128)(2,1)S(1)}, bf16[24,4096]{1,0:T(8,128)(2,1)}, u32[]{:S(2)}, u32[]{:S(2)}) collective-permute-start(bf16[24,4096]{1,0:T(8,128)(2,1)S(1)} %collective-permute-done.6.refs_1_), channel_id=1, source_target_pairs={{0,1},{1,0},{2,3},{3,2},{4,5},{5,4},{6,7},{7,6},{8,9},{9,8},{10,11... | collective-permute-start | bytes 589832 | tf_op jit(solution)/shard_map/ppermute | solution.py:64
  34.3 5.7 %collective-permute-start.13 = (bf16[24,4096]{1,0:T(8,128)(2,1)S(1)}, bf16[24,4096]{1,0:T(8,128)(2,1)S(1)}, u32[]{:S(2)}, u32[]{:S(2)}) collective-permute-start(bf16[24,4096]{1,0:T(8,128)(2,1)S(1)} %collective-permute-done.9.refs_4_), channel_id=1, source_target_pairs={{0,4},{1,3},{4,8},{5,1},{8,12},{9,5},{12,14},{13,9},{14,10},{15,13... | collective-permute-start | bytes 589832 | tf_op jit(solution)/shard_map/ppermute | solution.py:49
  36.4 3.6 %collective-permute-start.12 = (bf16[24,4096]{1,0:T(8,128)(2,1)S(1)}, bf16[24,4096]{1,0:T(8,128)(2,1)S(1)}, u32[]{:S(2)}, u32[]{:S(2)}) collective-permute-start(bf16[24,4096]{1,0:T(8,128)(2,1)S(1)} %collective-permute-done.10.refs_5_), channel_id=1, source_target_pairs={{0,1},{1,0},{2,3},{3,2},{4,5},{5,4},{6,7},{7,6},{8,9},{9,8},{10,11... | collective-permute-start | bytes 589832 | tf_op jit(solution)/shard_map/ppermute | solution.py:64
  36.4 3.6 %collective-permute-start.11 = (bf16[24,4096]{1,0:T(8,128)(2,1)S(1)}, bf16[24,4096]{1,0:T(8,128)(2,1)S(1)}, u32[]{:S(2)}, u32[]{:S(2)}) collective-permute-start(bf16[24,4096]{1,0:T(8,128)(2,1)S(1)} %collective-permute-done.9.refs_4_), channel_id=1, source_target_pairs={{0,1},{1,0},{2,3},{3,2},{4,5},{5,4},{6,7},{7,6},{8,9},{9,8},{10,11... | collective-permute-start | bytes 589832 | tf_op jit(solution)/shard_map/ppermute | solution.py:64
  40.0 3.6 %collective-permute-start.14 = (bf16[24,4096]{1,0:T(8,128)(2,1)S(1)}, bf16[24,4096]{1,0:T(8,128)(2,1)S(1)}, u32[]{:S(2)}, u32[]{:S(2)}) collective-permute-start(bf16[24,4096]{1,0:T(8,128)(2,1)S(1)} %collective-permute-done.13.refs_0_), channel_id=1, source_target_pairs={{0,1},{1,0},{2,3},{3,2},{4,5},{5,4},{6,7},{7,6},{8,9},{9,8},{10,11... | collective-permute-start | bytes 589832 | tf_op jit(solution)/shard_map/ppermute | solution.py:64
  43.5 2.0 %copy-start.2 = (s32[2,32,4]{1,2,0:T(4,128)S(1)}, s32[2,32,4]{1,2,0:T(4,128)}, u32[]{:S(2)}) copy-start(s32[2,32,4]{1,2,0:T(4,128)} %param.27) | copy-start | bytes 3076
  43.5 2.0 %copy-start.3 = (bf16[4,768]{1,0:T(4,128)(2,1)S(1)}, bf16[4,768]{1,0:T(4,128)(2,1)}, u32[]{:S(2)}) copy-start(bf16[4,768]{1,0:T(4,128)(2,1)} %rest_0_.1) | copy-start | bytes 18436
  43.5 2.0 %copy-start.4 = (bf16[768]{0:T(1024)(128)(2,1)S(1)}, bf16[768]{0:T(1024)(128)(2,1)}, u32[]{:S(2)}) copy-start(bf16[768]{0:T(1024)(128)(2,1)} %rest_1_.1) | copy-start | bytes 4612
  43.6 2.0 %copy-start.5 = (bf16[256]{0:T(256)(128)(2,1)S(1)}, bf16[256]{0:T(256)(128)(2,1)}, u32[]{:S(2)}) copy-start(bf16[256]{0:T(256)(128)(2,1)} %rest_2_.1) | copy-start | bytes 1540
  45.6 5.1 %copy-start = (bf16[256,4096]{1,0:T(8,128)(2,1)S(1)}, bf16[256,4096]{1,0:T(8,128)(2,1)}, u32[]{:S(2)}) copy-start(bf16[256,4096]{1,0:T(8,128)(2,1)} %weight_ref.1) | copy-start | bytes 6291460
  50.2 2.2 %collective-permute-start.15 = (bf16[192,256]{1,0:T(8,128)(2,1)S(1)}, bf16[192,256]{1,0:T(8,128)(2,1)S(1)}, u32[]{:S(2)}, u32[]{:S(2)}) collective-permute-start(bf16[192,256]{1,0:T(8,128)(2,1)S(1)} %get-tuple-element.39), channel_id=1, source_target_pairs={{0,1},{1,0},{2,3},{3,2},{4,5},{5,4},{6,7},{7,6},{8,9},{9,8},{10,11... | collective-permute-start | bytes 294920 | tf_op jit(solution)/shard_map/ppermute | solution.py:64
  53.7 5.7 %collective-permute-start.17 = (bf16[24,4096]{1,0:T(8,128)(2,1)S(1)}, bf16[24,4096]{1,0:T(8,128)(2,1)S(1)}, u32[]{:S(2)}, u32[]{:S(2)}) collective-permute-start(bf16[24,4096]{1,0:T(8,128)(2,1)S(1)} %get-tuple-element.41), channel_id=1, source_target_pairs={{0,4},{1,3},{4,8},{5,1},{8,12},{9,5},{12,14},{13,9},{14,10},{15,13... | collective-permute-start | bytes 589832 | tf_op jit(solution)/shard_map/ppermute | solution.py:49
  55.9 5.8 %collective-permute-start.21 = (bf16[24,4096]{1,0:T(8,128)(2,1)S(1)}, bf16[24,4096]{1,0:T(8,128)(2,1)S(1)}, u32[]{:S(2)}, u32[]{:S(2)}) collective-permute-start(bf16[24,4096]{1,0:T(8,128)(2,1)S(1)} %get-tuple-element.42), channel_id=1, source_target_pairs={{0,4},{1,3},{4,8},{5,1},{8,12},{9,5},{12,14},{13,9},{14,10},{15,13... | collective-permute-start | bytes 589832 | tf_op jit(solution)/shard_map/ppermute | solution.py:49
  59.5 5.7 %collective-permute-start.18 = (bf16[24,4096]{1,0:T(8,128)(2,1)S(1)}, bf16[24,4096]{1,0:T(8,128)(2,1)S(1)}, u32[]{:S(2)}, u32[]{:S(2)}) collective-permute-start(bf16[24,4096]{1,0:T(8,128)(2,1)S(1)} %onward.6), channel_id=1, source_target_pairs={{0,4},{1,3},{4,8},{5,1},{8,12},{9,5},{12,14},{13,9},{14,10},{15,13... | collective-permute-start | bytes 589832 | tf_op jit(solution)/shard_map/ppermute | solution.py:49
  61.7 5.7 %collective-permute-start.22 = (bf16[24,4096]{1,0:T(8,128)(2,1)S(1)}, bf16[24,4096]{1,0:T(8,128)(2,1)S(1)}, u32[]{:S(2)}, u32[]{:S(2)}) collective-permute-start(bf16[24,4096]{1,0:T(8,128)(2,1)S(1)} %onward.9), channel_id=1, source_target_pairs={{0,4},{1,3},{4,8},{5,1},{8,12},{9,5},{12,14},{13,9},{14,10},{15,13... | collective-permute-start | bytes 589832 | tf_op jit(solution)/shard_map/ppermute | solution.py:49
  65.3 5.7 %collective-permute-start.19 = (bf16[24,4096]{1,0:T(8,128)(2,1)S(1)}, bf16[24,4096]{1,0:T(8,128)(2,1)S(1)}, u32[]{:S(2)}, u32[]{:S(2)}) collective-permute-start(bf16[24,4096]{1,0:T(8,128)(2,1)S(1)} %onward.7), channel_id=1, source_target_pairs={{0,4},{1,3},{4,8},{5,1},{8,12},{9,5},{12,14},{13,9},{14,10},{15,13... | collective-permute-start | bytes 589832 | tf_op jit(solution)/shard_map/ppermute | solution.py:49
  67.4 5.7 %collective-permute-start.23 = (bf16[24,4096]{1,0:T(8,128)(2,1)S(1)}, bf16[24,4096]{1,0:T(8,128)(2,1)S(1)}, u32[]{:S(2)}, u32[]{:S(2)}) collective-permute-start(bf16[24,4096]{1,0:T(8,128)(2,1)S(1)} %onward.10), channel_id=1, source_target_pairs={{0,4},{1,3},{4,8},{5,1},{8,12},{9,5},{12,14},{13,9},{14,10},{15,13... | collective-permute-start | bytes 589832 | tf_op jit(solution)/shard_map/ppermute | solution.py:49
  71.0 5.7 %collective-permute-start.20 = (bf16[24,4096]{1,0:T(8,128)(2,1)S(1)}, bf16[24,4096]{1,0:T(8,128)(2,1)S(1)}, u32[]{:S(2)}, u32[]{:S(2)}) collective-permute-start(bf16[24,4096]{1,0:T(8,128)(2,1)S(1)} %onward.8), channel_id=1, source_target_pairs={{0,4},{1,3},{4,8},{5,1},{8,12},{9,5},{12,14},{13,9},{14,10},{15,13... | collective-permute-start | bytes 589832 | tf_op jit(solution)/shard_map/ppermute | solution.py:49
  73.2 3.6 %collective-permute-start.24 = (bf16[24,4096]{1,0:T(8,128)(2,1)S(1)}, bf16[24,4096]{1,0:T(8,128)(2,1)S(1)}, u32[]{:S(2)}, u32[]{:S(2)}) collective-permute-start(bf16[24,4096]{1,0:T(8,128)(2,1)S(1)} %collective-permute-done.23), channel_id=1, source_target_pairs={{0,1},{1,0},{2,3},{3,2},{4,5},{5,4},{6,7},{7,6},{8,9},{9,8},{10,11... | collective-permute-start | bytes 589832 | tf_op jit(solution)/shard_map/ppermute | solution.py:64
where the time goes:
time: 77.8 us; the launch traced here: 77.5 us
  starting transfers between devices  34.3 us (44%)
  Pallas kernels  27.8 us (36%)
  waiting for transfers between devices  11.5 us (15%)
  other arithmetic  1.51 us (2%)
  local copies, waits for them, and re-layouts  1.5 us (2%)
  between operations  0.85 us (1%)
    ppermute x13, starting transfers between devices, stream(): return lax.ppermute(array, 'dp', pairs)  24.8 us
    pallas_call x13, Pallas kernels, kernel_call(): pl.pallas_call(kernel, out_shape=outs, in_specs=[scalars] * smem + [whole...  18.3 us
    ppermute x13, waiting for transfers between devices, stream(): return lax.ppermute(array, 'dp', pairs)  10.5 us
    all_to_all x1, starting transfers between devices, body(): lax.all_to_all(offered, 'dp', split_axis=0, concat_axis=0, tiled=True)  6.32 us
    pallas_call x1, Pallas kernels, early_stage(): pl.pallas_call(functools.partial(early_kernel, count, tile), out_shape=ja...  6.13 us
    pallas_call x1, Pallas kernels, load(): pl.pallas_call(load_kernel, out_shape=[jax.ShapeDtypeStruct(a.shape, a.dt...  3.4 us
    ppermute x11, starting transfers between devices, other_core(): lax.ppermute(array, 'dp', [(d, d ^ 1) for d in range(2 * chip_count)])  2.56 us
  transfers between devices with their start and end apart: 26, of which 6 were waited for; matrix products, arithmetic and copies ran while one was open for 3% of the time, Pallas kernels for 33%

commit v1 on v0

--- a/solution.py
+++ b/solution.py
@@ -232,7 +232,7 @@
     hbm = pl.BlockSpec(memory_space=pltpu.HBM)
     return pl.pallas_call(
         functools.partial(early_kernel, count, tile),
-        out_shape=jax.ShapeDtypeStruct((rows * count, width + 128), jnp.float32),
+        out_shape=pltpu.HBM((rows * count, width + 128), jnp.float32),
         in_specs=[whole] * count + [hbm, whole],
         out_specs=hbm,
         scratch_shapes=[
@@ -250,9 +250,11 @@
 
 
 def part_kernel(mine_ref, weight_ref, out_ref):
+    rows = out_ref.shape[0]
+
     def body(columns):
         out_ref[:, columns] = jnp.dot(
-            mine_ref[...], weight_ref[:, columns], preferred_element_type=jnp.float32
+            mine_ref[:rows, :], weight_ref[:, columns], preferred_element_type=jnp.float32
         )
 
     column_tiles(out_ref.shape[1], body)
@@ -269,9 +271,12 @@
     column_tiles(held_ref.shape[1], body)
 
 
-def rest_kernel(rows, part_ref, theirs_ref, held_ref, out_ref):
+def rest_kernel(rows, mine_ref, theirs_ref, weight_ref, held_ref, out_ref):
     def body(columns):
-        out_ref[:, columns] = part_ref[2 * rows :, columns] + jnp.dot(
+        total = jnp.dot(
+            mine_ref[2 * rows :, :], weight_ref[:, columns], preferred_element_type=jnp.float32
+        )
+        out_ref[:, columns] = total + jnp.dot(
             theirs_ref[2 * rows :, :], held_ref[:, columns], preferred_element_type=jnp.float32
         )
 
@@ -612,7 +617,7 @@
     block = jax.ShapeDtypeStruct((rows_dev, width), jnp.bfloat16)
     part = kernel_call(
         part_kernel,
-        jax.ShapeDtypeStruct((total_rows, width), jnp.float32),
+        jax.ShapeDtypeStruct((2 * rows_dev, width), jnp.float32),
         [mine, out_weight],
         [],
         "sums_part",
@@ -631,7 +636,7 @@
     shares = kernel_call(
         functools.partial(rest_kernel, rows_dev),
         jax.ShapeDtypeStruct((total_rows - 2 * rows_dev, width), jnp.float32),
-        [part, theirs, held],
+        [mine, theirs, out_weight, held],
         [],
         "sums_rest",
         flops=1 << 30,

time: 77.8 us -> 77.4 us (level)
  local copies, waits for them, and re-layouts: 1.5 us -> 0.65 us
    unnamed x13 -> x11, local copies, waits for them, and re-layouts: 1.5 us -> 0.65 us
  transfers between devices with their start and end apart: 26 -> 26, of which waited for: 6 -> 6; matrix products, arithmetic and copies ran while one was open for 3% -> 3% of each run, Pallas kernels for 33% -> 34%
where the time goes in v1:
time: 77.4 us; the launch traced here: 77 us
  starting transfers between devices  34.6 us (45%)
  Pallas kernels  28.4 us (37%)
  waiting for transfers between devices  11.1 us (14%)
  other arithmetic  1.51 us (2%)
  between operations  0.85 us (1%)
    ppermute x13, starting transfers between devices, stream(): return lax.ppermute(array, 'dp', pairs)  25 us
    pallas_call x13, Pallas kernels, kernel_call(): pl.pallas_call(kernel, out_shape=outs, in_specs=[scalars] * smem + [whole...  18.2 us
    ppermute x13, waiting for transfers between devices, stream(): return lax.ppermute(array, 'dp', pairs)  10.1 us
    pallas_call x1, Pallas kernels, early_stage(): pl.pallas_call(functools.partial(early_kernel, count, tile), out_shape=pl...  6.76 us
    all_to_all x1, starting transfers between devices, body(): lax.all_to_all(offered, 'dp', split_axis=0, concat_axis=0, tiled=True)  6.32 us
    pallas_call x1, Pallas kernels, load(): pl.pallas_call(load_kernel, out_shape=[jax.ShapeDtypeStruct(a.shape, a.dt...  3.4 us
    ppermute x11, starting transfers between devices, other_core(): lax.ppermute(array, 'dp', [(d, d ^ 1) for d in range(2 * chip_count)])  2.55 us
  transfers between devices with their start and end apart: 26, of which 6 were waited for; matrix products, arithmetic and copies ran while one was open for 3% of the time, Pallas kernels for 34%

profile of v1, /device:TPU:0, one launch (start us, length us, event | category | flops | bytes accessed | tf_op | source)
XLA Modules:
  0.0 77.0 jit_solution(17722184642780278488)
XLA Ops:
  0.6 3.1 %collective-permute-start = (bf16[24,4096]{1,0:T(8,128)(2,1)}, bf16[24,4096]{1,0:T(8,128)(2,1)S(1)}, u32[]{:S(2)}, u32[]{:S(2)}) collective-permute-start(bf16[24,4096]{1,0:T(8,128)(2,1)} %refs_0_.1), channel_id=1, source_target_pairs={{0,4},{1,3},{4,8},{5,1},{8,12},{9,5},{12,14},{13,9},{14,10},{15,13... | collective-permute-start | bytes 589832 | tf_op jit(solution)/shard_map/ppermute | solution.py:49
  3.7 0.7 collective-permute-start.1
  4.4 2.7 %offer_pages.1 = bf16[16,80,128]{2,1,0:T(8,128)(2,1)} custom-call(s32[1]{0:T(128)} %bitcast.my_ref, s32[2,4,32]{2,1,0:T(4,128)} %bitcast.3, bf16[32,32,128]{2,1,0:T(8,128)(2,1)} %state_ref.1, bf16[3,32,96]{2,1,0:T(8,128)(2,1)} %bitcast.5), custom_call_target="tpu_custom_call" | custom-call | bytes 8388608 | tf_op jit(solution)/shard_map/offer_pages/pallas_call | solution.py:71
  7.1 0.7 pad_add_fusion.scalar_ref
  7.9 0.8 pad_maximum_fusion.number_ref
  8.6 0.0 collective-permute-done.refs_2_
  8.6 1.0 %collective-permute-done.1.refs_3_ = bf16[24,4096]{1,0:T(8,128)(2,1)S(1)} collective-permute-done((bf16[24,4096]{1,0:T(8,128)(2,1)}, bf16[24,4096]{1,0:T(8,128)(2,1)S(1)}, u32[]{:S(2)}, u32[]{:S(2)}) %collective-permute-start.1) | collective-permute-done | bytes 196640 | tf_op jit(solution)/shard_map/ppermute | solution.py:60
  9.6 0.1 collective-permute-start.16
  9.7 6.3 %all-to-all-start = ((bf16[16,80,128]{2,1,0:T(8,128)(2,1)}), bf16[16,80,128]{2,1,0:T(8,128)(2,1)S(1)}, u32[]{:S(2)}, u32[]{:S(2)}) async-start(bf16[16,80,128]{2,1,0:T(8,128)(2,1)} %offer_pages.1), calls=%async_computation | async-start | bytes 655360 | tf_op jit(solution)/shard_map/all_to_all | solution.py:547
  16.1 0.4 collective-permute-start.3
  16.5 0.2 collective-permute-start.4
  16.6 0.3 collective-permute-start.5
  17.0 1.7 %collective-permute-start.2 = (bf16[24,4096]{1,0:T(8,128)(2,1)S(1)}, bf16[24,4096]{1,0:T(8,128)(2,1)S(1)}, u32[]{:S(2)}, u32[]{:S(2)}) collective-permute-start(bf16[24,4096]{1,0:T(8,128)(2,1)S(1)} %collective-permute-done.refs_2_), channel_id=1, source_target_pairs={{0,4},{1,3},{4,8},{5,1},{8,12},{9,5},{12,14},{13,9},{14,10},{15,13... | collective-permute-start | bytes 589832 | tf_op jit(solution)/shard_map/ppermute | solution.py:49
  18.6 0.0 collective-permute-done.3.refs_1_
  18.6 1.5 %collective-permute-start.6 = (bf16[24,4096]{1,0:T(8,128)(2,1)S(1)}, bf16[24,4096]{1,0:T(8,128)(2,1)S(1)}, u32[]{:S(2)}, u32[]{:S(2)}) collective-permute-start(bf16[24,4096]{1,0:T(8,128)(2,1)S(1)} %collective-permute-done.1.refs_3_), channel_id=1, source_target_pairs={{0,4},{1,3},{4,8},{5,1},{8,12},{9,5},{12,14},{13,9},{14,10},{15,13... | collective-permute-start | bytes 589832 | tf_op jit(solution)/shard_map/ppermute | solution.py:49
  20.1 0.0 collective-permute-done.4.refs_4_
  20.1 0.0 collective-permute-done.5.refs_5_
  20.1 6.8 %early_stage.1.rest_3_ = f32[144,1152]{1,0:T(8,128)} custom-call(bf16[24,4096]{1,0:T(8,128)(2,1)} %refs_0_.1, bf16[24,4096]{1,0:T(8,128)(2,1)S(1)} %collective-permute-done.3.refs_1_, bf16[24,4096]{1,0:T(8,128)(2,1)S(1)} %collective-permute-done.refs_2_, bf16[24,4096]{1,0:T(8,128)(2,1)S(1)} %collective-permute-done.1.refs_3_, ...), custom_call_target="tpu_custom_call" | custom-call | flops 2147483648 | bytes 8388608 | tf_op jit(solution)/shard_map/early_stage/pallas_call | solution.py:233
  26.9 0.0 collective-permute-done.2.refs_0_
  26.9 1.5 %collective-permute-start.9 = (bf16[24,4096]{1,0:T(8,128)(2,1)S(1)}, bf16[24,4096]{1,0:T(8,128)(2,1)S(1)}, u32[]{:S(2)}, u32[]{:S(2)}) collective-permute-start(bf16[24,4096]{1,0:T(8,128)(2,1)S(1)} %collective-permute-done.2.refs_0_), channel_id=1, source_target_pairs={{0,4},{1,3},{4,8},{5,1},{8,12},{9,5},{12,14},{13,9},{14,10},{15,13... | collective-permute-start | bytes 589832 | tf_op jit(solution)/shard_map/ppermute | solution.py:49
  28.4 1.9 %collective-permute-start.10 = (bf16[24,4096]{1,0:T(8,128)(2,1)S(1)}, bf16[24,4096]{1,0:T(8,128)(2,1)S(1)}, u32[]{:S(2)}, u32[]{:S(2)}) collective-permute-start(bf16[24,4096]{1,0:T(8,128)(2,1)S(1)} %collective-permute-done.6.refs_1_), channel_id=1, source_target_pairs={{0,4},{1,3},{4,8},{5,1},{8,12},{9,5},{12,14},{13,9},{14,10},{15,13... | collective-permute-start | bytes 589832 | tf_op jit(solution)/shard_map/ppermute | solution.py:49
  30.3 0.5 collective-permute-start.8
  30.9 0.0 all-to-all-done.page_ref
  30.9 3.4 %load.1 = (bf16[4096,1024]{1,0:T(8,128)(2,1)S(1)}, bf16[2,4096]{1,0:T(2,128)(2,1)S(1)}) custom-call(bf16[4096,1024]{1,0:T(8,128)(2,1)} %refs_0_.2, bf16[2,4096]{1,0:T(2,128)(2,1)} %refs_1_), custom_call_target="tpu_custom_call" | custom-call | bytes 8388608 | tf_op jit(solution)/shard_map/load/pallas_call | solution.py:142
  34.3 0.0 collective-permute-done.9.refs_4_
  34.3 2.2 %collective-permute-start.13 = (bf16[24,4096]{1,0:T(8,128)(2,1)S(1)}, bf16[24,4096]{1,0:T(8,128)(2,1)S(1)}, u32[]{:S(2)}, u32[]{:S(2)}) collective-permute-start(bf16[24,4096]{1,0:T(8,128)(2,1)S(1)} %collective-permute-done.9.refs_4_), channel_id=1, source_target_pairs={{0,4},{1,3},{4,8},{5,1},{8,12},{9,5},{12,14},{13,9},{14,10},{15,13... | collective-permute-start | bytes 589832 | tf_op jit(solution)/shard_map/ppermute | solution.py:49
  36.4 0.0 collective-permute-done.7.refs_2_
  36.4 0.5 collective-permute-start.11
  37.0 3.0 %collective-permute-done.13.refs_0_ = bf16[24,4096]{1,0:T(8,128)(2,1)S(1)} collective-permute-done((bf16[24,4096]{1,0:T(8,128)(2,1)S(1)}, bf16[24,4096]{1,0:T(8,128)(2,1)S(1)}, u32[]{:S(2)}, u32[]{:S(2)}) %collective-permute-start.13) | collective-permute-done | bytes 196640 | tf_op jit(solution)/shard_map/ppermute | solution.py:49
  40.0 0.0 collective-permute-start.14
  40.0 0.0 collective-permute-done.8.refs_3_
  40.0 3.5 %stage.2.rest_4_ = f32[192,1152]{1,0:T(8,128)S(1)} custom-call(bf16[24,4096]{1,0:T(8,128)(2,1)S(1)} %collective-permute-done.2.refs_0_, bf16[24,4096]{1,0:T(8,128)(2,1)S(1)} %collective-permute-done.6.refs_1_, bf16[24,4096]{1,0:T(8,128)(2,1)S(1)} %collective-permute-done.7.refs_2_, bf16[24,4096]{1,0:T(8,128)(2,1)} %collective-permute-done.8.refs_3_, ...), custom_call_target="tpu_custom_call" | custom-call | flops 2415919104 | bytes 8388608 | tf_op jit(solution)/shard_map/stage/pallas_call | solution.py:71
  43.5 0.0 copy-start.1
  43.5 0.0 copy-start.2
  43.5 0.0 copy-start.3
  43.6 0.0 copy-start.4
  43.6 0.0 collective-permute-done.14.refs_1_
  43.6 1.9 %stage.3.rest_5_ = f32[48,1152]{1,0:T(8,128)S(1)} custom-call(bf16[24,4096]{1,0:T(8,128)(2,1)S(1)} %collective-permute-done.13.refs_0_, bf16[24,4096]{1,0:T(8,128)(2,1)S(1)} %collective-permute-done.14.refs_1_, bf16[4096,1024]{1,0:T(8,128)(2,1)S(1)} %get-tuple-element.36.refs_8_.refs_2_, bf16[2,4096]{1,0:T(2,128)(2,1)S(1)} %get-tuple-element.37.refs_9_.refs_3_), custom_call_target="tpu_custom_call" | custom-call | flops 2415919104 | bytes 8388608 | tf_op jit(solution)/shard_map/stage/pallas_call | solution.py:71
  45.5 0.0 copy-done.1
  45.6 0.0 copy-start
  45.6 4.6 %mixer.1 = (f32[2,2,128,128]{3,2,1,0:T(8,128)}, bf16[2,3,768]{2,1,0:T(4,128)(2,1)S(1)}, bf16[192,256]{1,0:T(8,128)(2,1)S(1)}, bf16[192,256]{1,0:T(8,128)(2,1)S(1)}) custom-call(s32[19]{0:T(128)S(1)} %pad_add_fusion.scalar_ref, s32[2,4,32]{2,1,0:T(4,128)S(1)} %bitcast.4, f32[6]{0:T(128)S(1)} %pad_maximum_fusion.number_ref, ...), custom_call_target="tpu_custom_call" | custom-call | flops 1073741824 | bytes 8388608 | tf_op jit(solution)/shard_map/mixer/pallas_call | solution.py:71
  50.2 0.5 collective-permute-start.15
  50.7 1.3 %sums_part.1.part_ref = f32[48,4096]{1,0:T(8,128)S(1)} custom-call(bf16[192,256]{1,0:T(8,128)(2,1)S(1)} %get-tuple-element.38.mine_ref, bf16[256,4096]{1,0:T(8,128)(2,1)S(1)} %copy-done), custom_call_target="tpu_custom_call" | custom-call | flops 1073741824 | bytes 8388608 | tf_op jit(solution)/shard_map/sums_part/pallas_call | solution.py:71
  51.9 0.0 collective-permute-done.15.theirs_ref
  52.0 0.0 collective-permute-done.16.held_ref
  52.0 1.3 %sums_first.1 = (bf16[24,4096]{1,0:T(8,128)(2,1)S(1)}, bf16[24,4096]{1,0:T(8,128)(2,1)S(1)}) custom-call(f32[48,4096]{1,0:T(8,128)S(1)} %sums_part.1.part_ref, bf16[192,256]{1,0:T(8,128)(2,1)S(1)} %collective-permute-done.15.theirs_ref, bf16[256,4096]{1,0:T(8,128)(2,1)S(1)} %collective-permute-done.16.held_ref), custom_call_target="tpu_custom_call" | custom-call | flops 1073741824 | bytes 8388608 | tf_op jit(solution)/shard_map/sums_first/pallas_call | solution.py:71
  53.3 2.2 %collective-permute-start.17 = (bf16[24,4096]{1,0:T(8,128)(2,1)S(1)}, bf16[24,4096]{1,0:T(8,128)(2,1)S(1)}, u32[]{:S(2)}, u32[]{:S(2)}) collective-permute-start(bf16[24,4096]{1,0:T(8,128)(2,1)S(1)} %get-tuple-element.41), channel_id=1, source_target_pairs={{0,4},{1,3},{4,8},{5,1},{8,12},{9,5},{12,14},{13,9},{14,10},{15,13... | collective-permute-start | bytes 589832 | tf_op jit(solution)/shard_map/ppermute | solution.py:49
  55.4 0.5 collective-permute-start.21
  55.9 2.0 %sums_rest.1.share_ref = f32[144,4096]{1,0:T(8,128)S(1)} custom-call(bf16[192,256]{1,0:T(8,128)(2,1)S(1)} %get-tuple-element.38.mine_ref, bf16[192,256]{1,0:T(8,128)(2,1)S(1)} %collective-permute-done.15.theirs_ref, bf16[256,4096]{1,0:T(8,128)(2,1)S(1)} %copy-done, bf16[256,4096]{1,0:T(8,128)(2,1)S(1)} %collective-permute-done.16.held_ref), custom_call_target="tpu_custom_call" | custom-call | flops 1073741824 | bytes 8388608 | tf_op jit(solution)/shard_map/sums_rest/pallas_call | solution.py:71
  57.9 1.1 %collective-permute-done.17.refs_0_ = bf16[24,4096]{1,0:T(8,128)(2,1)S(1)} collective-permute-done((bf16[24,4096]{1,0:T(8,128)(2,1)S(1)}, bf16[24,4096]{1,0:T(8,128)(2,1)S(1)}, u32[]{:S(2)}, u32[]{:S(2)}) %collective-permute-start.17) | collective-permute-done | bytes 196640 | tf_op jit(solution)/shard_map/ppermute | solution.py:49
  59.1 2.2 %collective-permute-start.18 = (bf16[24,4096]{1,0:T(8,128)(2,1)S(1)}, bf16[24,4096]{1,0:T(8,128)(2,1)S(1)}, u32[]{:S(2)}, u32[]{:S(2)}) collective-permute-start(bf16[24,4096]{1,0:T(8,128)(2,1)S(1)} %onward.6), channel_id=1, source_target_pairs={{0,4},{1,3},{4,8},{5,1},{8,12},{9,5},{12,14},{13,9},{14,10},{15,13... | collective-permute-start | bytes 589832 | tf_op jit(solution)/shard_map/ppermute | solution.py:49
  61.2 0.0 collective-permute-done.21.refs_0_
  61.3 2.1 %collective-permute-start.22 = (bf16[24,4096]{1,0:T(8,128)(2,1)S(1)}, bf16[24,4096]{1,0:T(8,128)(2,1)S(1)}, u32[]{:S(2)}, u32[]{:S(2)}) collective-permute-start(bf16[24,4096]{1,0:T(8,128)(2,1)S(1)} %onward.9), channel_id=1, source_target_pairs={{0,4},{1,3},{4,8},{5,1},{8,12},{9,5},{12,14},{13,9},{14,10},{15,13... | collective-permute-start | bytes 589832 | tf_op jit(solution)/shard_map/ppermute | solution.py:49
  63.3 1.5 %collective-permute-done.18.refs_0_ = bf16[24,4096]{1,0:T(8,128)(2,1)S(1)} collective-permute-done((bf16[24,4096]{1,0:T(8,128)(2,1)S(1)}, bf16[24,4096]{1,0:T(8,128)(2,1)S(1)}, u32[]{:S(2)}, u32[]{:S(2)}) %collective-permute-start.18) | collective-permute-done | bytes 196640 | tf_op jit(solution)/shard_map/ppermute | solution.py:49
  64.8 2.2 %collective-permute-start.19 = (bf16[24,4096]{1,0:T(8,128)(2,1)S(1)}, bf16[24,4096]{1,0:T(8,128)(2,1)S(1)}, u32[]{:S(2)}, u32[]{:S(2)}) collective-permute-start(bf16[24,4096]{1,0:T(8,128)(2,1)S(1)} %onward.7), channel_id=1, source_target_pairs={{0,4},{1,3},{4,8},{5,1},{8,12},{9,5},{12,14},{13,9},{14,10},{15,13... | collective-permute-start | bytes 589832 | tf_op jit(solution)/shard_map/ppermute | solution.py:49
  67.0 0.0 collective-permute-done.22.refs_0_
  67.0 2.1 %collective-permute-start.23 = (bf16[24,4096]{1,0:T(8,128)(2,1)S(1)}, bf16[24,4096]{1,0:T(8,128)(2,1)S(1)}, u32[]{:S(2)}, u32[]{:S(2)}) collective-permute-start(bf16[24,4096]{1,0:T(8,128)(2,1)S(1)} %onward.10), channel_id=1, source_target_pairs={{0,4},{1,3},{4,8},{5,1},{8,12},{9,5},{12,14},{13,9},{14,10},{15,13... | collective-permute-start | bytes 589832 | tf_op jit(solution)/shard_map/ppermute | solution.py:49
  69.1 1.5 %collective-permute-done.19.refs_0_ = bf16[24,4096]{1,0:T(8,128)(2,1)S(1)} collective-permute-done((bf16[24,4096]{1,0:T(8,128)(2,1)S(1)}, bf16[24,4096]{1,0:T(8,128)(2,1)S(1)}, u32[]{:S(2)}, u32[]{:S(2)}) %collective-permute-start.19) | collective-permute-done | bytes 196640 | tf_op jit(solution)/shard_map/ppermute | solution.py:49
  70.6 2.2 %collective-permute-start.20 = (bf16[24,4096]{1,0:T(8,128)(2,1)S(1)}, bf16[24,4096]{1,0:T(8,128)(2,1)S(1)}, u32[]{:S(2)}, u32[]{:S(2)}) collective-permute-start(bf16[24,4096]{1,0:T(8,128)(2,1)S(1)} %onward.8), channel_id=1, source_target_pairs={{0,4},{1,3},{4,8},{5,1},{8,12},{9,5},{12,14},{13,9},{14,10},{15,13... | collective-permute-start | bytes 589832 | tf_op jit(solution)/shard_map/ppermute | solution.py:49
  72.7 0.0 collective-permute-done.23
  72.7 0.0 collective-permute-start.24
  72.7 0.6 copy.18
  73.3 3.0 %collective-permute-done.20.refs_0_ = bf16[24,4096]{1,0:T(8,128)(2,1)S(1)} collective-permute-done((bf16[24,4096]{1,0:T(8,128)(2,1)S(1)}, bf16[24,4096]{1,0:T(8,128)(2,1)S(1)}, u32[]{:S(2)}, u32[]{:S(2)}) %collective-permute-start.20) | collective-permute-done | bytes 196640 | tf_op jit(solution)/shard_map/ppermute | solution.py:49
  76.3 0.7 onward.11
  (16 shorter events, 0.2 us)
Async XLA Ops:
  0.6 8.0 %collective-permute-start = (bf16[24,4096]{1,0:T(8,128)(2,1)}, bf16[24,4096]{1,0:T(8,128)(2,1)S(1)}, u32[]{:S(2)}, u32[]{:S(2)}) collective-permute-start(bf16[24,4096]{1,0:T(8,128)(2,1)} %refs_0_.1), channel_id=1, source_target_pairs={{0,4},{1,3},{4,8},{5,1},{8,12},{9,5},{12,14},{13,9},{14,10},{15,13... | collective-permute-start | bytes 589832 | tf_op jit(solution)/shard_map/ppermute | solution.py:49
  3.7 5.9 %collective-permute-start.1 = (bf16[24,4096]{1,0:T(8,128)(2,1)}, bf16[24,4096]{1,0:T(8,128)(2,1)S(1)}, u32[]{:S(2)}, u32[]{:S(2)}) collective-permute-start(bf16[24,4096]{1,0:T(8,128)(2,1)} %refs_0_.1), channel_id=1, source_target_pairs={{1,4},{0,3},{5,8},{4,1},{9,12},{8,5},{13,14},{12,9},{15,10},{14,13... | collective-permute-start | bytes 589832 | tf_op jit(solution)/shard_map/ppermute | solution.py:60
  9.6 42.4 %collective-permute-start.16 = (bf16[256,4096]{1,0:T(8,128)(2,1)}, bf16[256,4096]{1,0:T(8,128)(2,1)S(1)}, u32[]{:S(2)}, u32[]{:S(2)}) collective-permute-start(bf16[256,4096]{1,0:T(8,128)(2,1)} %weight_ref.3), channel_id=1, source_target_pairs={{0,1},{1,0},{2,3},{3,2},{4,5},{5,4},{6,7},{7,6},{8,9},{9,8},{10,11... | collective-permute-start | bytes 6291464 | tf_op jit(solution)/shard_map/ppermute | solution.py:64
  9.7 21.1 %all-to-all-start = ((bf16[16,80,128]{2,1,0:T(8,128)(2,1)}), bf16[16,80,128]{2,1,0:T(8,128)(2,1)S(1)}, u32[]{:S(2)}, u32[]{:S(2)}) async-start(bf16[16,80,128]{2,1,0:T(8,128)(2,1)} %offer_pages.1), calls=%async_computation | async-start | bytes 655360 | tf_op jit(solution)/shard_map/all_to_all | solution.py:547
  16.1 2.6 %collective-permute-start.3 = (bf16[24,4096]{1,0:T(8,128)(2,1)}, bf16[24,4096]{1,0:T(8,128)(2,1)S(1)}, u32[]{:S(2)}, u32[]{:S(2)}) collective-permute-start(bf16[24,4096]{1,0:T(8,128)(2,1)} %refs_0_.1), channel_id=1, source_target_pairs={{0,1},{1,0},{2,3},{3,2},{4,5},{5,4},{6,7},{7,6},{8,9},{9,8},{10,11... | collective-permute-start | bytes 589832 | tf_op jit(solution)/shard_map/ppermute | solution.py:64
  16.5 3.6 %collective-permute-start.4 = (bf16[24,4096]{1,0:T(8,128)(2,1)S(1)}, bf16[24,4096]{1,0:T(8,128)(2,1)S(1)}, u32[]{:S(2)}, u32[]{:S(2)}) collective-permute-start(bf16[24,4096]{1,0:T(8,128)(2,1)S(1)} %collective-permute-done.refs_2_), channel_id=1, source_target_pairs={{0,1},{1,0},{2,3},{3,2},{4,5},{5,4},{6,7},{7,6},{8,9},{9,8},{10,11... | collective-permute-start | bytes 589832 | tf_op jit(solution)/shard_map/ppermute | solution.py:64
  16.6 3.5 %collective-permute-start.5 = (bf16[24,4096]{1,0:T(8,128)(2,1)S(1)}, bf16[24,4096]{1,0:T(8,128)(2,1)S(1)}, u32[]{:S(2)}, u32[]{:S(2)}) collective-permute-start(bf16[24,4096]{1,0:T(8,128)(2,1)S(1)} %collective-permute-done.1.refs_3_), channel_id=1, source_target_pairs={{0,1},{1,0},{2,3},{3,2},{4,5},{5,4},{6,7},{7,6},{8,9},{9,8},{10,11... | collective-permute-start | bytes 589832 | tf_op jit(solution)/shard_map/ppermute | solution.py:64
  17.0 9.9 %collective-permute-start.2 = (bf16[24,4096]{1,0:T(8,128)(2,1)S(1)}, bf16[24,4096]{1,0:T(8,128)(2,1)S(1)}, u32[]{:S(2)}, u32[]{:S(2)}) collective-permute-start(bf16[24,4096]{1,0:T(8,128)(2,1)S(1)} %collective-permute-done.refs_2_), channel_id=1, source_target_pairs={{0,4},{1,3},{4,8},{5,1},{8,12},{9,5},{12,14},{13,9},{14,10},{15,13... | collective-permute-start | bytes 589832 | tf_op jit(solution)/shard_map/ppermute | solution.py:49
  18.6 9.8 %collective-permute-start.6 = (bf16[24,4096]{1,0:T(8,128)(2,1)S(1)}, bf16[24,4096]{1,0:T(8,128)(2,1)S(1)}, u32[]{:S(2)}, u32[]{:S(2)}) collective-permute-start(bf16[24,4096]{1,0:T(8,128)(2,1)S(1)} %collective-permute-done.1.refs_3_), channel_id=1, source_target_pairs={{0,4},{1,3},{4,8},{5,1},{8,12},{9,5},{12,14},{13,9},{14,10},{15,13... | collective-permute-start | bytes 589832 | tf_op jit(solution)/shard_map/ppermute | solution.py:49
  26.9 7.4 %collective-permute-start.9 = (bf16[24,4096]{1,0:T(8,128)(2,1)S(1)}, bf16[24,4096]{1,0:T(8,128)(2,1)S(1)}, u32[]{:S(2)}, u32[]{:S(2)}) collective-permute-start(bf16[24,4096]{1,0:T(8,128)(2,1)S(1)} %collective-permute-done.2.refs_0_), channel_id=1, source_target_pairs={{0,4},{1,3},{4,8},{5,1},{8,12},{9,5},{12,14},{13,9},{14,10},{15,13... | collective-permute-start | bytes 589832 | tf_op jit(solution)/shard_map/ppermute | solution.py:49
  28.4 8.0 %collective-permute-start.10 = (bf16[24,4096]{1,0:T(8,128)(2,1)S(1)}, bf16[24,4096]{1,0:T(8,128)(2,1)S(1)}, u32[]{:S(2)}, u32[]{:S(2)}) collective-permute-start(bf16[24,4096]{1,0:T(8,128)(2,1)S(1)} %collective-permute-done.6.refs_1_), channel_id=1, source_target_pairs={{0,4},{1,3},{4,8},{5,1},{8,12},{9,5},{12,14},{13,9},{14,10},{15,13... | collective-permute-start | bytes 589832 | tf_op jit(solution)/shard_map/ppermute | solution.py:49
  30.3 6.1 %collective-permute-start.7 = (bf16[24,4096]{1,0:T(8,128)(2,1)S(1)}, bf16[24,4096]{1,0:T(8,128)(2,1)S(1)}, u32[]{:S(2)}, u32[]{:S(2)}) collective-permute-start(bf16[24,4096]{1,0:T(8,128)(2,1)S(1)} %collective-permute-done.2.refs_0_), channel_id=1, source_target_pairs={{0,1},{1,0},{2,3},{3,2},{4,5},{5,4},{6,7},{7,6},{8,9},{9,8},{10,11... | collective-permute-start | bytes 589832 | tf_op jit(solution)/shard_map/ppermute | solution.py:64
  30.3 9.7 %collective-permute-start.8 = (bf16[24,4096]{1,0:T(8,128)(2,1)S(1)}, bf16[24,4096]{1,0:T(8,128)(2,1)}, u32[]{:S(2)}, u32[]{:S(2)}) collective-permute-start(bf16[24,4096]{1,0:T(8,128)(2,1)S(1)} %collective-permute-done.6.refs_1_), channel_id=1, source_target_pairs={{0,1},{1,0},{2,3},{3,2},{4,5},{5,4},{6,7},{7,6},{8,9},{9,8},{10,11... | collective-permute-start | bytes 589832 | tf_op jit(solution)/shard_map/ppermute | solution.py:64
  34.3 5.7 %collective-permute-start.13 = (bf16[24,4096]{1,0:T(8,128)(2,1)S(1)}, bf16[24,4096]{1,0:T(8,128)(2,1)S(1)}, u32[]{:S(2)}, u32[]{:S(2)}) collective-permute-start(bf16[24,4096]{1,0:T(8,128)(2,1)S(1)} %collective-permute-done.9.refs_4_), channel_id=1, source_target_pairs={{0,4},{1,3},{4,8},{5,1},{8,12},{9,5},{12,14},{13,9},{14,10},{15,13... | collective-permute-start | bytes 589832 | tf_op jit(solution)/shard_map/ppermute | solution.py:49
  36.4 3.6 %collective-permute-start.12 = (bf16[24,4096]{1,0:T(8,128)(2,1)S(1)}, bf16[24,4096]{1,0:T(8,128)(2,1)S(1)}, u32[]{:S(2)}, u32[]{:S(2)}) collective-permute-start(bf16[24,4096]{1,0:T(8,128)(2,1)S(1)} %collective-permute-done.10.refs_5_), channel_id=1, source_target_pairs={{0,1},{1,0},{2,3},{3,2},{4,5},{5,4},{6,7},{7,6},{8,9},{9,8},{10,11... | collective-permute-start | bytes 589832 | tf_op jit(solution)/shard_map/ppermute | solution.py:64
  36.4 3.6 %collective-permute-start.11 = (bf16[24,4096]{1,0:T(8,128)(2,1)S(1)}, bf16[24,4096]{1,0:T(8,128)(2,1)S(1)}, u32[]{:S(2)}, u32[]{:S(2)}) collective-permute-start(bf16[24,4096]{1,0:T(8,128)(2,1)S(1)} %collective-permute-done.9.refs_4_), channel_id=1, source_target_pairs={{0,1},{1,0},{2,3},{3,2},{4,5},{5,4},{6,7},{7,6},{8,9},{9,8},{10,11... | collective-permute-start | bytes 589832 | tf_op jit(solution)/shard_map/ppermute | solution.py:64
  40.0 3.6 %collective-permute-start.14 = (bf16[24,4096]{1,0:T(8,128)(2,1)S(1)}, bf16[24,4096]{1,0:T(8,128)(2,1)S(1)}, u32[]{:S(2)}, u32[]{:S(2)}) collective-permute-start(bf16[24,4096]{1,0:T(8,128)(2,1)S(1)} %collective-permute-done.13.refs_0_), channel_id=1, source_target_pairs={{0,1},{1,0},{2,3},{3,2},{4,5},{5,4},{6,7},{7,6},{8,9},{9,8},{10,11... | collective-permute-start | bytes 589832 | tf_op jit(solution)/shard_map/ppermute | solution.py:64
  43.5 2.0 %copy-start.1 = (s32[2,32,4]{1,2,0:T(4,128)S(1)}, s32[2,32,4]{1,2,0:T(4,128)}, u32[]{:S(2)}) copy-start(s32[2,32,4]{1,2,0:T(4,128)} %param.27) | copy-start | bytes 3076
  43.5 2.0 %copy-start.2 = (bf16[4,768]{1,0:T(4,128)(2,1)S(1)}, bf16[4,768]{1,0:T(4,128)(2,1)}, u32[]{:S(2)}) copy-start(bf16[4,768]{1,0:T(4,128)(2,1)} %rest_0_.1) | copy-start | bytes 18436
  43.5 2.0 %copy-start.3 = (bf16[768]{0:T(1024)(128)(2,1)S(1)}, bf16[768]{0:T(1024)(128)(2,1)}, u32[]{:S(2)}) copy-start(bf16[768]{0:T(1024)(128)(2,1)} %rest_1_.1) | copy-start | bytes 4612
  43.6 2.0 %copy-start.4 = (bf16[256]{0:T(256)(128)(2,1)S(1)}, bf16[256]{0:T(256)(128)(2,1)}, u32[]{:S(2)}) copy-start(bf16[256]{0:T(256)(128)(2,1)} %rest_2_.1) | copy-start | bytes 1540
  45.6 5.1 %copy-start = (bf16[256,4096]{1,0:T(8,128)(2,1)S(1)}, bf16[256,4096]{1,0:T(8,128)(2,1)}, u32[]{:S(2)}) copy-start(bf16[256,4096]{1,0:T(8,128)(2,1)} %weight_ref.3) | copy-start | bytes 6291460
  50.2 1.8 %collective-permute-start.15 = (bf16[192,256]{1,0:T(8,128)(2,1)S(1)}, bf16[192,256]{1,0:T(8,128)(2,1)S(1)}, u32[]{:S(2)}, u32[]{:S(2)}) collective-permute-start(bf16[192,256]{1,0:T(8,128)(2,1)S(1)} %get-tuple-element.39), channel_id=1, source_target_pairs={{0,1},{1,0},{2,3},{3,2},{4,5},{5,4},{6,7},{7,6},{8,9},{9,8},{10,11... | collective-permute-start | bytes 294920 | tf_op jit(solution)/shard_map/ppermute | solution.py:64
  53.3 5.7 %collective-permute-start.17 = (bf16[24,4096]{1,0:T(8,128)(2,1)S(1)}, bf16[24,4096]{1,0:T(8,128)(2,1)S(1)}, u32[]{:S(2)}, u32[]{:S(2)}) collective-permute-start(bf16[24,4096]{1,0:T(8,128)(2,1)S(1)} %get-tuple-element.41), channel_id=1, source_target_pairs={{0,4},{1,3},{4,8},{5,1},{8,12},{9,5},{12,14},{13,9},{14,10},{15,13... | collective-permute-start | bytes 589832 | tf_op jit(solution)/shard_map/ppermute | solution.py:49
  55.4 5.8 %collective-permute-start.21 = (bf16[24,4096]{1,0:T(8,128)(2,1)S(1)}, bf16[24,4096]{1,0:T(8,128)(2,1)S(1)}, u32[]{:S(2)}, u32[]{:S(2)}) collective-permute-start(bf16[24,4096]{1,0:T(8,128)(2,1)S(1)} %get-tuple-element.42), channel_id=1, source_target_pairs={{0,4},{1,3},{4,8},{5,1},{8,12},{9,5},{12,14},{13,9},{14,10},{15,13... | collective-permute-start | bytes 589832 | tf_op jit(solution)/shard_map/ppermute | solution.py:49
  59.1 5.7 %collective-permute-start.18 = (bf16[24,4096]{1,0:T(8,128)(2,1)S(1)}, bf16[24,4096]{1,0:T(8,128)(2,1)S(1)}, u32[]{:S(2)}, u32[]{:S(2)}) collective-permute-start(bf16[24,4096]{1,0:T(8,128)(2,1)S(1)} %onward.6), channel_id=1, source_target_pairs={{0,4},{1,3},{4,8},{5,1},{8,12},{9,5},{12,14},{13,9},{14,10},{15,13... | collective-permute-start | bytes 589832 | tf_op jit(solution)/shard_map/ppermute | solution.py:49
  61.3 5.7 %collective-permute-start.22 = (bf16[24,4096]{1,0:T(8,128)(2,1)S(1)}, bf16[24,4096]{1,0:T(8,128)(2,1)S(1)}, u32[]{:S(2)}, u32[]{:S(2)}) collective-permute-start(bf16[24,4096]{1,0:T(8,128)(2,1)S(1)} %onward.9), channel_id=1, source_target_pairs={{0,4},{1,3},{4,8},{5,1},{8,12},{9,5},{12,14},{13,9},{14,10},{15,13... | collective-permute-start | bytes 589832 | tf_op jit(solution)/shard_map/ppermute | solution.py:49
  64.8 5.7 %collective-permute-start.19 = (bf16[24,4096]{1,0:T(8,128)(2,1)S(1)}, bf16[24,4096]{1,0:T(8,128)(2,1)S(1)}, u32[]{:S(2)}, u32[]{:S(2)}) collective-permute-start(bf16[24,4096]{1,0:T(8,128)(2,1)S(1)} %onward.7), channel_id=1, source_target_pairs={{0,4},{1,3},{4,8},{5,1},{8,12},{9,5},{12,14},{13,9},{14,10},{15,13... | collective-permute-start | bytes 589832 | tf_op jit(solution)/shard_map/ppermute | solution.py:49
  67.0 5.7 %collective-permute-start.23 = (bf16[24,4096]{1,0:T(8,128)(2,1)S(1)}, bf16[24,4096]{1,0:T(8,128)(2,1)S(1)}, u32[]{:S(2)}, u32[]{:S(2)}) collective-permute-start(bf16[24,4096]{1,0:T(8,128)(2,1)S(1)} %onward.10), channel_id=1, source_target_pairs={{0,4},{1,3},{4,8},{5,1},{8,12},{9,5},{12,14},{13,9},{14,10},{15,13... | collective-permute-start | bytes 589832 | tf_op jit(solution)/shard_map/ppermute | solution.py:49
  70.6 5.7 %collective-permute-start.20 = (bf16[24,4096]{1,0:T(8,128)(2,1)S(1)}, bf16[24,4096]{1,0:T(8,128)(2,1)S(1)}, u32[]{:S(2)}, u32[]{:S(2)}) collective-permute-start(bf16[24,4096]{1,0:T(8,128)(2,1)S(1)} %onward.8), channel_id=1, source_target_pairs={{0,4},{1,3},{4,8},{5,1},{8,12},{9,5},{12,14},{13,9},{14,10},{15,13... | collective-permute-start | bytes 589832 | tf_op jit(solution)/shard_map/ppermute | solution.py:49
  72.7 3.6 %collective-permute-start.24 = (bf16[24,4096]{1,0:T(8,128)(2,1)S(1)}, bf16[24,4096]{1,0:T(8,128)(2,1)S(1)}, u32[]{:S(2)}, u32[]{:S(2)}) collective-permute-start(bf16[24,4096]{1,0:T(8,128)(2,1)S(1)} %collective-permute-done.23), channel_id=1, source_target_pairs={{0,1},{1,0},{2,3},{3,2},{4,5},{5,4},{6,7},{7,6},{8,9},{9,8},{10,11... | collective-permute-start | bytes 589832 | tf_op jit(solution)/shard_map/ppermute | solution.py:64

commit v2 on v1

--- a/solution.py
+++ b/solution.py
@@ -568,12 +568,12 @@
             other_core(own_type, chip_count),
             other_core(other_type, chip_count),
         ]
-        if len(pending) >= 6 or step == half - 1:
+        if len(pending) >= max(4, half) and step < half - 1:
             staged.append(stage(pending, weight_here, rates_here))
             pending = []
     own_type = stream(own_type, chip_count)
     last = [own_type, other_core(own_type, chip_count)]
-    staged.append(stage(last, weight_here, rates_here))
+    staged.append(stage(pending + last, weight_here, rates_here))
 
     live_rows = SPAN - BLK
     normed_rows = jax.ShapeDtypeStruct((chip_count * rows_dev, heads_dev * HEAD_DIM), jnp.bfloat16)

time: 77.4 us -> 77.6 us (level)
  waiting for transfers between devices: 11.1 us -> 13.7 us
  Pallas kernels: 28.4 us -> 27 us
  starting transfers between devices: 34.6 us -> 33.7 us
    ppermute x13, waiting for transfers between devices: 10.1 us -> 12.7 us  [stream(): return lax.ppermute(array, 'dp', pairs)]
    pallas_call x13, Pallas kernels: 18.2 us -> 16.8 us  [kernel_call(): pl.pallas_call(kernel, out_shape=outs, in_specs=[scalars] * smem + [whole...]
  transfers between devices with their start and end apart: 26 -> 26, of which waited for: 6 -> 7; matrix products, arithmetic and copies ran while one was open for 3% -> 3% of each run, Pallas kernels for 34% -> 32%
where the time goes in v2:
time: 77.6 us; the launch traced here: 77.3 us
  starting transfers between devices  33.7 us (43%)
  Pallas kernels  27 us (35%)
  waiting for transfers between devices  13.7 us (18%)
  other arithmetic  1.51 us (2%)
  between operations  0.86 us (1%)
    ppermute x13, starting transfers between devices, stream(): return lax.ppermute(array, 'dp', pairs)  24.5 us
    pallas_call x13, Pallas kernels, kernel_call(): pl.pallas_call(kernel, out_shape=outs, in_specs=[scalars] * smem + [whole...  16.8 us
    ppermute x13, waiting for transfers between devices, stream(): return lax.ppermute(array, 'dp', pairs)  12.7 us
    pallas_call x1, Pallas kernels, early_stage(): pl.pallas_call(functools.partial(early_kernel, count, tile), out_shape=pl...  6.76 us
    all_to_all x1, starting transfers between devices, body(): lax.all_to_all(offered, 'dp', split_axis=0, concat_axis=0, tiled=True)  6.32 us
    pallas_call x1, Pallas kernels, load(): pl.pallas_call(load_kernel, out_shape=[jax.ShapeDtypeStruct(a.shape, a.dt...  3.4 us
    ppermute x11, starting transfers between devices, other_core(): lax.ppermute(array, 'dp', [(d, d ^ 1) for d in range(2 * chip_count)])  2.13 us
  transfers between devices with their start and end apart: 26, of which 7 were waited for; matrix products, arithmetic and copies ran while one was open for 3% of the time, Pallas kernels for 32%

profile of v2, /device:TPU:0, one launch (start us, length us, event | category | flops | bytes accessed | tf_op | source)
XLA Modules:
  0.0 77.3 jit_solution(6626704976548103829)
XLA Ops:
  0.6 3.1 %collective-permute-start = (bf16[24,4096]{1,0:T(8,128)(2,1)}, bf16[24,4096]{1,0:T(8,128)(2,1)S(1)}, u32[]{:S(2)}, u32[]{:S(2)}) collective-permute-start(bf16[24,4096]{1,0:T(8,128)(2,1)} %refs_0_.1), channel_id=1, source_target_pairs={{0,4},{1,3},{4,8},{5,1},{8,12},{9,5},{12,14},{13,9},{14,10},{15,13... | collective-permute-start | bytes 589832 | tf_op jit(solution)/shard_map/ppermute | solution.py:49
  3.7 0.7 collective-permute-start.1
  4.4 2.7 %offer_pages.1 = bf16[16,80,128]{2,1,0:T(8,128)(2,1)} custom-call(s32[1]{0:T(128)} %bitcast.my_ref, s32[2,4,32]{2,1,0:T(4,128)} %bitcast.3, bf16[32,32,128]{2,1,0:T(8,128)(2,1)} %state_ref.1, bf16[3,32,96]{2,1,0:T(8,128)(2,1)} %bitcast.5), custom_call_target="tpu_custom_call" | custom-call | bytes 8388608 | tf_op jit(solution)/shard_map/offer_pages/pallas_call | solution.py:71
  7.1 0.7 pad_add_fusion.scalar_ref
  7.9 0.8 pad_maximum_fusion.number_ref
  8.6 0.0 collective-permute-done.refs_2_
  8.6 1.0 %collective-permute-done.1.refs_3_ = bf16[24,4096]{1,0:T(8,128)(2,1)S(1)} collective-permute-done((bf16[24,4096]{1,0:T(8,128)(2,1)}, bf16[24,4096]{1,0:T(8,128)(2,1)S(1)}, u32[]{:S(2)}, u32[]{:S(2)}) %collective-permute-start.1) | collective-permute-done | bytes 196640 | tf_op jit(solution)/shard_map/ppermute | solution.py:60
  9.6 0.1 collective-permute-start.16
  9.7 6.3 %all-to-all-start = ((bf16[16,80,128]{2,1,0:T(8,128)(2,1)}), bf16[16,80,128]{2,1,0:T(8,128)(2,1)S(1)}, u32[]{:S(2)}, u32[]{:S(2)}) async-start(bf16[16,80,128]{2,1,0:T(8,128)(2,1)} %offer_pages.1), calls=%async_computation | async-start | bytes 655360 | tf_op jit(solution)/shard_map/all_to_all | solution.py:547
  16.1 0.4 collective-permute-start.3
  16.5 0.2 collective-permute-start.4
  16.6 0.3 collective-permute-start.5
  17.0 1.7 %collective-permute-start.2 = (bf16[24,4096]{1,0:T(8,128)(2,1)S(1)}, bf16[24,4096]{1,0:T(8,128)(2,1)S(1)}, u32[]{:S(2)}, u32[]{:S(2)}) collective-permute-start(bf16[24,4096]{1,0:T(8,128)(2,1)S(1)} %collective-permute-done.refs_2_), channel_id=1, source_target_pairs={{0,4},{1,3},{4,8},{5,1},{8,12},{9,5},{12,14},{13,9},{14,10},{15,13... | collective-permute-start | bytes 589832 | tf_op jit(solution)/shard_map/ppermute | solution.py:49
  18.6 0.0 collective-permute-done.3.refs_1_
  18.6 1.5 %collective-permute-start.6 = (bf16[24,4096]{1,0:T(8,128)(2,1)S(1)}, bf16[24,4096]{1,0:T(8,128)(2,1)S(1)}, u32[]{:S(2)}, u32[]{:S(2)}) collective-permute-start(bf16[24,4096]{1,0:T(8,128)(2,1)S(1)} %collective-permute-done.1.refs_3_), channel_id=1, source_target_pairs={{0,4},{1,3},{4,8},{5,1},{8,12},{9,5},{12,14},{13,9},{14,10},{15,13... | collective-permute-start | bytes 589832 | tf_op jit(solution)/shard_map/ppermute | solution.py:49
  20.1 6.8 %early_stage.1.rest_3_ = f32[144,1152]{1,0:T(8,128)} custom-call(bf16[24,4096]{1,0:T(8,128)(2,1)} %refs_0_.1, bf16[24,4096]{1,0:T(8,128)(2,1)S(1)} %collective-permute-done.3.refs_1_, bf16[24,4096]{1,0:T(8,128)(2,1)S(1)} %collective-permute-done.refs_2_, bf16[24,4096]{1,0:T(8,128)(2,1)S(1)} %collective-permute-done.1.refs_3_, ...), custom_call_target="tpu_custom_call" | custom-call | flops 2147483648 | bytes 8388608 | tf_op jit(solution)/shard_map/early_stage/pallas_call | solution.py:233
  26.9 0.0 collective-permute-done.2.refs_0_
  26.9 1.5 %collective-permute-start.9 = (bf16[24,4096]{1,0:T(8,128)(2,1)S(1)}, bf16[24,4096]{1,0:T(8,128)(2,1)S(1)}, u32[]{:S(2)}, u32[]{:S(2)}) collective-permute-start(bf16[24,4096]{1,0:T(8,128)(2,1)S(1)} %collective-permute-done.2.refs_0_), channel_id=1, source_target_pairs={{0,4},{1,3},{4,8},{5,1},{8,12},{9,5},{12,14},{13,9},{14,10},{15,13... | collective-permute-start | bytes 589832 | tf_op jit(solution)/shard_map/ppermute | solution.py:49
  28.4 0.0 collective-permute-start.7
  28.4 0.0 collective-permute-done.6.refs_1_
  28.4 1.9 %collective-permute-start.10 = (bf16[24,4096]{1,0:T(8,128)(2,1)S(1)}, bf16[24,4096]{1,0:T(8,128)(2,1)S(1)}, u32[]{:S(2)}, u32[]{:S(2)}) collective-permute-start(bf16[24,4096]{1,0:T(8,128)(2,1)S(1)} %collective-permute-done.6.refs_1_), channel_id=1, source_target_pairs={{0,4},{1,3},{4,8},{5,1},{8,12},{9,5},{12,14},{13,9},{14,10},{15,13... | collective-permute-start | bytes 589832 | tf_op jit(solution)/shard_map/ppermute | solution.py:49
  30.3 0.0 all-to-all-done.page_ref
  30.4 3.4 %load.1 = (bf16[4096,1024]{1,0:T(8,128)(2,1)S(1)}, bf16[2,4096]{1,0:T(2,128)(2,1)S(1)}) custom-call(bf16[4096,1024]{1,0:T(8,128)(2,1)} %refs_0_.2, bf16[2,4096]{1,0:T(2,128)(2,1)} %refs_1_), custom_call_target="tpu_custom_call" | custom-call | bytes 8388608 | tf_op jit(solution)/shard_map/load/pallas_call | solution.py:142
  33.8 0.0 collective-permute-done.9.refs_0_
  33.8 2.2 %collective-permute-start.13 = (bf16[24,4096]{1,0:T(8,128)(2,1)S(1)}, bf16[24,4096]{1,0:T(8,128)(2,1)S(1)}, u32[]{:S(2)}, u32[]{:S(2)}) collective-permute-start(bf16[24,4096]{1,0:T(8,128)(2,1)S(1)} %collective-permute-done.9.refs_0_), channel_id=1, source_target_pairs={{0,4},{1,3},{4,8},{5,1},{8,12},{9,5},{12,14},{13,9},{14,10},{15,13... | collective-permute-start | bytes 589832 | tf_op jit(solution)/shard_map/ppermute | solution.py:49
  35.9 0.0 collective-permute-done.10.refs_1_
  35.9 0.5 collective-permute-start.12
  36.4 0.0 collective-permute-done.7.refs_2_
  36.4 0.1 collective-permute-start.11
  36.5 3.0 %collective-permute-done.13.refs_4_ = bf16[24,4096]{1,0:T(8,128)(2,1)S(1)} collective-permute-done((bf16[24,4096]{1,0:T(8,128)(2,1)S(1)}, bf16[24,4096]{1,0:T(8,128)(2,1)S(1)}, u32[]{:S(2)}, u32[]{:S(2)}) %collective-permute-start.13) | collective-permute-done | bytes 196640 | tf_op jit(solution)/shard_map/ppermute | solution.py:49
  39.5 0.0 collective-permute-start.14
  39.5 0.0 collective-permute-done.8.refs_3_
  39.5 2.0 %stage.2.rest_4_ = f32[96,1152]{1,0:T(8,128)S(1)} custom-call(bf16[24,4096]{1,0:T(8,128)(2,1)S(1)} %collective-permute-done.2.refs_0_, bf16[24,4096]{1,0:T(8,128)(2,1)S(1)} %collective-permute-done.6.refs_1_, bf16[24,4096]{1,0:T(8,128)(2,1)S(1)} %collective-permute-done.7.refs_2_, bf16[24,4096]{1,0:T(8,128)(2,1)S(1)} %collective-permute-done.8.refs_3_, ...), custom_call_target="tpu_custom_call" | custom-call | flops 2415919104 | bytes 8388608 | tf_op jit(solution)/shard_map/stage/pallas_call | solution.py:71
  41.5 0.0 copy-start.1
  41.5 0.0 copy-start.2
  41.5 0.0 copy-start.3
  41.5 0.0 copy-start.4
  41.5 0.0 collective-permute-done.12.refs_3_
  41.5 2.1 %stage.3.rest_5_ = f32[144,1152]{1,0:T(8,128)S(1)} custom-call(bf16[24,4096]{1,0:T(8,128)(2,1)S(1)} %collective-permute-done.9.refs_0_, bf16[24,4096]{1,0:T(8,128)(2,1)S(1)} %collective-permute-done.10.refs_1_, bf16[24,4096]{1,0:T(8,128)(2,1)S(1)} %collective-permute-done.11.refs_2_, bf16[24,4096]{1,0:T(8,128)(2,1)S(1)} %collective-permute-done.12.refs_3_, ...), custom_call_target="tpu_custom_call" | custom-call | flops 2415919104 | bytes 8388608 | tf_op jit(solution)/shard_map/stage/pallas_call | solution.py:71
  43.6 0.0 copy-start
  43.7 4.6 %mixer.1 = (f32[2,2,128,128]{3,2,1,0:T(8,128)}, bf16[2,3,768]{2,1,0:T(4,128)(2,1)S(1)}, bf16[192,256]{1,0:T(8,128)(2,1)S(1)}, bf16[192,256]{1,0:T(8,128)(2,1)S(1)}) custom-call(s32[19]{0:T(128)S(1)} %pad_add_fusion.scalar_ref, s32[2,4,32]{2,1,0:T(4,128)S(1)} %bitcast.4, f32[6]{0:T(128)S(1)} %pad_maximum_fusion.number_ref, ...), custom_call_target="tpu_custom_call" | custom-call | flops 1073741824 | bytes 8388608 | tf_op jit(solution)/shard_map/mixer/pallas_call | solution.py:71
  48.3 0.5 collective-permute-start.15
  48.8 1.3 %sums_part.1.part_ref = f32[48,4096]{1,0:T(8,128)S(1)} custom-call(bf16[192,256]{1,0:T(8,128)(2,1)S(1)} %get-tuple-element.38.mine_ref, bf16[256,4096]{1,0:T(8,128)(2,1)S(1)} %copy-done), custom_call_target="tpu_custom_call" | custom-call | flops 1073741824 | bytes 8388608 | tf_op jit(solution)/shard_map/sums_part/pallas_call | solution.py:71
  50.0 0.0 collective-permute-done.15.theirs_ref
  50.1 0.0 collective-permute-done.16.held_ref
  50.1 1.3 %sums_first.1 = (bf16[24,4096]{1,0:T(8,128)(2,1)S(1)}, bf16[24,4096]{1,0:T(8,128)(2,1)S(1)}) custom-call(f32[48,4096]{1,0:T(8,128)S(1)} %sums_part.1.part_ref, bf16[192,256]{1,0:T(8,128)(2,1)S(1)} %collective-permute-done.15.theirs_ref, bf16[256,4096]{1,0:T(8,128)(2,1)S(1)} %collective-permute-done.16.held_ref), custom_call_target="tpu_custom_call" | custom-call | flops 1073741824 | bytes 8388608 | tf_op jit(solution)/shard_map/sums_first/pallas_call | solution.py:71
  51.4 2.1 %collective-permute-start.21 = (bf16[24,4096]{1,0:T(8,128)(2,1)S(1)}, bf16[24,4096]{1,0:T(8,128)(2,1)S(1)}, u32[]{:S(2)}, u32[]{:S(2)}) collective-permute-start(bf16[24,4096]{1,0:T(8,128)(2,1)S(1)} %get-tuple-element.42), channel_id=1, source_target_pairs={{0,4},{1,3},{4,8},{5,1},{8,12},{9,5},{12,14},{13,9},{14,10},{15,13... | collective-permute-start | bytes 589832 | tf_op jit(solution)/shard_map/ppermute | solution.py:49
  53.5 0.1 collective-permute-start.17
  53.6 2.0 %sums_rest.1.share_ref = f32[144,4096]{1,0:T(8,128)S(1)} custom-call(bf16[192,256]{1,0:T(8,128)(2,1)S(1)} %get-tuple-element.38.mine_ref, bf16[192,256]{1,0:T(8,128)(2,1)S(1)} %collective-permute-done.15.theirs_ref, bf16[256,4096]{1,0:T(8,128)(2,1)S(1)} %copy-done, bf16[256,4096]{1,0:T(8,128)(2,1)S(1)} %collective-permute-done.16.held_ref), custom_call_target="tpu_custom_call" | custom-call | flops 1073741824 | bytes 8388608 | tf_op jit(solution)/shard_map/sums_rest/pallas_call | solution.py:71
  55.6 1.5 %collective-permute-done.21.refs_0_ = bf16[24,4096]{1,0:T(8,128)(2,1)S(1)} collective-permute-done((bf16[24,4096]{1,0:T(8,128)(2,1)S(1)}, bf16[24,4096]{1,0:T(8,128)(2,1)S(1)}, u32[]{:S(2)}, u32[]{:S(2)}) %collective-permute-start.21) | collective-permute-done | bytes 196640 | tf_op jit(solution)/shard_map/ppermute | solution.py:49
  57.2 2.1 %collective-permute-start.22 = (bf16[24,4096]{1,0:T(8,128)(2,1)S(1)}, bf16[24,4096]{1,0:T(8,128)(2,1)S(1)}, u32[]{:S(2)}, u32[]{:S(2)}) collective-permute-start(bf16[24,4096]{1,0:T(8,128)(2,1)S(1)} %onward.9), channel_id=1, source_target_pairs={{0,4},{1,3},{4,8},{5,1},{8,12},{9,5},{12,14},{13,9},{14,10},{15,13... | collective-permute-start | bytes 589832 | tf_op jit(solution)/shard_map/ppermute | solution.py:49
  59.3 2.1 %collective-permute-start.18 = (bf16[24,4096]{1,0:T(8,128)(2,1)S(1)}, bf16[24,4096]{1,0:T(8,128)(2,1)S(1)}, u32[]{:S(2)}, u32[]{:S(2)}) collective-permute-start(bf16[24,4096]{1,0:T(8,128)(2,1)S(1)} %onward.6), channel_id=1, source_target_pairs={{0,4},{1,3},{4,8},{5,1},{8,12},{9,5},{12,14},{13,9},{14,10},{15,13... | collective-permute-start | bytes 589832 | tf_op jit(solution)/shard_map/ppermute | solution.py:49
  61.4 1.5 %collective-permute-done.22.refs_0_ = bf16[24,4096]{1,0:T(8,128)(2,1)S(1)} collective-permute-done((bf16[24,4096]{1,0:T(8,128)(2,1)S(1)}, bf16[24,4096]{1,0:T(8,128)(2,1)S(1)}, u32[]{:S(2)}, u32[]{:S(2)}) %collective-permute-start.22) | collective-permute-done | bytes 196640 | tf_op jit(solution)/shard_map/ppermute | solution.py:49
  62.9 2.1 %collective-permute-start.23 = (bf16[24,4096]{1,0:T(8,128)(2,1)S(1)}, bf16[24,4096]{1,0:T(8,128)(2,1)S(1)}, u32[]{:S(2)}, u32[]{:S(2)}) collective-permute-start(bf16[24,4096]{1,0:T(8,128)(2,1)S(1)} %onward.10), channel_id=1, source_target_pairs={{0,4},{1,3},{4,8},{5,1},{8,12},{9,5},{12,14},{13,9},{14,10},{15,13... | collective-permute-start | bytes 589832 | tf_op jit(solution)/shard_map/ppermute | solution.py:49
  65.1 0.0 collective-permute-done.18.refs_0_
  65.1 2.1 %collective-permute-start.19 = (bf16[24,4096]{1,0:T(8,128)(2,1)S(1)}, bf16[24,4096]{1,0:T(8,128)(2,1)S(1)}, u32[]{:S(2)}, u32[]{:S(2)}) collective-permute-start(bf16[24,4096]{1,0:T(8,128)(2,1)S(1)} %onward.7), channel_id=1, source_target_pairs={{0,4},{1,3},{4,8},{5,1},{8,12},{9,5},{12,14},{13,9},{14,10},{15,13... | collective-permute-start | bytes 589832 | tf_op jit(solution)/shard_map/ppermute | solution.py:49
  67.2 1.5 %collective-permute-done.23 = bf16[24,4096]{1,0:T(8,128)(2,1)S(1)} collective-permute-done((bf16[24,4096]{1,0:T(8,128)(2,1)S(1)}, bf16[24,4096]{1,0:T(8,128)(2,1)S(1)}, u32[]{:S(2)}, u32[]{:S(2)}) %collective-permute-start.23) | collective-permute-done | bytes 196640 | tf_op jit(solution)/shard_map/ppermute | solution.py:49
  68.6 0.0 collective-permute-start.24
  68.6 2.2 %collective-permute-done.19.refs_0_ = bf16[24,4096]{1,0:T(8,128)(2,1)S(1)} collective-permute-done((bf16[24,4096]{1,0:T(8,128)(2,1)S(1)}, bf16[24,4096]{1,0:T(8,128)(2,1)S(1)}, u32[]{:S(2)}, u32[]{:S(2)}) %collective-permute-start.19) | collective-permute-done | bytes 196640 | tf_op jit(solution)/shard_map/ppermute | solution.py:49
  70.9 2.1 %collective-permute-start.20 = (bf16[24,4096]{1,0:T(8,128)(2,1)S(1)}, bf16[24,4096]{1,0:T(8,128)(2,1)S(1)}, u32[]{:S(2)}, u32[]{:S(2)}) collective-permute-start(bf16[24,4096]{1,0:T(8,128)(2,1)S(1)} %onward.8), channel_id=1, source_target_pairs={{0,4},{1,3},{4,8},{5,1},{8,12},{9,5},{12,14},{13,9},{14,10},{15,13... | collective-permute-start | bytes 589832 | tf_op jit(solution)/shard_map/ppermute | solution.py:49
  72.9 0.6 copy.18
  73.5 0.0 collective-permute-done.24.refs_1_
  73.5 3.0 %collective-permute-done.20.refs_0_ = bf16[24,4096]{1,0:T(8,128)(2,1)S(1)} collective-permute-done((bf16[24,4096]{1,0:T(8,128)(2,1)S(1)}, bf16[24,4096]{1,0:T(8,128)(2,1)S(1)}, u32[]{:S(2)}, u32[]{:S(2)}) %collective-permute-start.20) | collective-permute-done | bytes 196640 | tf_op jit(solution)/shard_map/ppermute | solution.py:49
  76.6 0.7 onward.11
  (16 shorter events, 0.2 us)
Async XLA Ops:
  0.6 8.0 %collective-permute-start = (bf16[24,4096]{1,0:T(8,128)(2,1)}, bf16[24,4096]{1,0:T(8,128)(2,1)S(1)}, u32[]{:S(2)}, u32[]{:S(2)}) collective-permute-start(bf16[24,4096]{1,0:T(8,128)(2,1)} %refs_0_.1), channel_id=1, source_target_pairs={{0,4},{1,3},{4,8},{5,1},{8,12},{9,5},{12,14},{13,9},{14,10},{15,13... | collective-permute-start | bytes 589832 | tf_op jit(solution)/shard_map/ppermute | solution.py:49
  3.7 5.9 %collective-permute-start.1 = (bf16[24,4096]{1,0:T(8,128)(2,1)}, bf16[24,4096]{1,0:T(8,128)(2,1)S(1)}, u32[]{:S(2)}, u32[]{:S(2)}) collective-permute-start(bf16[24,4096]{1,0:T(8,128)(2,1)} %refs_0_.1), channel_id=1, source_target_pairs={{1,4},{0,3},{5,8},{4,1},{9,12},{8,5},{13,14},{12,9},{15,10},{14,13... | collective-permute-start | bytes 589832 | tf_op jit(solution)/shard_map/ppermute | solution.py:60
  9.6 40.4 %collective-permute-start.16 = (bf16[256,4096]{1,0:T(8,128)(2,1)}, bf16[256,4096]{1,0:T(8,128)(2,1)S(1)}, u32[]{:S(2)}, u32[]{:S(2)}) collective-permute-start(bf16[256,4096]{1,0:T(8,128)(2,1)} %weight_ref.3), channel_id=1, source_target_pairs={{0,1},{1,0},{2,3},{3,2},{4,5},{5,4},{6,7},{7,6},{8,9},{9,8},{10,11... | collective-permute-start | bytes 6291464 | tf_op jit(solution)/shard_map/ppermute | solution.py:64
  9.7 20.6 %all-to-all-start = ((bf16[16,80,128]{2,1,0:T(8,128)(2,1)}), bf16[16,80,128]{2,1,0:T(8,128)(2,1)S(1)}, u32[]{:S(2)}, u32[]{:S(2)}) async-start(bf16[16,80,128]{2,1,0:T(8,128)(2,1)} %offer_pages.1), calls=%async_computation | async-start | bytes 655360 | tf_op jit(solution)/shard_map/all_to_all | solution.py:547
  16.1 2.6 %collective-permute-start.3 = (bf16[24,4096]{1,0:T(8,128)(2,1)}, bf16[24,4096]{1,0:T(8,128)(2,1)S(1)}, u32[]{:S(2)}, u32[]{:S(2)}) collective-permute-start(bf16[24,4096]{1,0:T(8,128)(2,1)} %refs_0_.1), channel_id=1, source_target_pairs={{0,1},{1,0},{2,3},{3,2},{4,5},{5,4},{6,7},{7,6},{8,9},{9,8},{10,11... | collective-permute-start | bytes 589832 | tf_op jit(solution)/shard_map/ppermute | solution.py:64
  16.5 3.6 %collective-permute-start.4 = (bf16[24,4096]{1,0:T(8,128)(2,1)S(1)}, bf16[24,4096]{1,0:T(8,128)(2,1)S(1)}, u32[]{:S(2)}, u32[]{:S(2)}) collective-permute-start(bf16[24,4096]{1,0:T(8,128)(2,1)S(1)} %collective-permute-done.refs_2_), channel_id=1, source_target_pairs={{0,1},{1,0},{2,3},{3,2},{4,5},{5,4},{6,7},{7,6},{8,9},{9,8},{10,11... | collective-permute-start | bytes 589832 | tf_op jit(solution)/shard_map/ppermute | solution.py:64
  16.6 3.5 %collective-permute-start.5 = (bf16[24,4096]{1,0:T(8,128)(2,1)S(1)}, bf16[24,4096]{1,0:T(8,128)(2,1)S(1)}, u32[]{:S(2)}, u32[]{:S(2)}) collective-permute-start(bf16[24,4096]{1,0:T(8,128)(2,1)S(1)} %collective-permute-done.1.refs_3_), channel_id=1, source_target_pairs={{0,1},{1,0},{2,3},{3,2},{4,5},{5,4},{6,7},{7,6},{8,9},{9,8},{10,11... | collective-permute-start | bytes 589832 | tf_op jit(solution)/shard_map/ppermute | solution.py:64
  17.0 9.9 %collective-permute-start.2 = (bf16[24,4096]{1,0:T(8,128)(2,1)S(1)}, bf16[24,4096]{1,0:T(8,128)(2,1)S(1)}, u32[]{:S(2)}, u32[]{:S(2)}) collective-permute-start(bf16[24,4096]{1,0:T(8,128)(2,1)S(1)} %collective-permute-done.refs_2_), channel_id=1, source_target_pairs={{0,4},{1,3},{4,8},{5,1},{8,12},{9,5},{12,14},{13,9},{14,10},{15,13... | collective-permute-start | bytes 589832 | tf_op jit(solution)/shard_map/ppermute | solution.py:49
  18.6 9.8 %collective-permute-start.6 = (bf16[24,4096]{1,0:T(8,128)(2,1)S(1)}, bf16[24,4096]{1,0:T(8,128)(2,1)S(1)}, u32[]{:S(2)}, u32[]{:S(2)}) collective-permute-start(bf16[24,4096]{1,0:T(8,128)(2,1)S(1)} %collective-permute-done.1.refs_3_), channel_id=1, source_target_pairs={{0,4},{1,3},{4,8},{5,1},{8,12},{9,5},{12,14},{13,9},{14,10},{15,13... | collective-permute-start | bytes 589832 | tf_op jit(solution)/shard_map/ppermute | solution.py:49
  26.9 6.9 %collective-permute-start.9 = (bf16[24,4096]{1,0:T(8,128)(2,1)S(1)}, bf16[24,4096]{1,0:T(8,128)(2,1)S(1)}, u32[]{:S(2)}, u32[]{:S(2)}) collective-permute-start(bf16[24,4096]{1,0:T(8,128)(2,1)S(1)} %collective-permute-done.2.refs_0_), channel_id=1, source_target_pairs={{0,4},{1,3},{4,8},{5,1},{8,12},{9,5},{12,14},{13,9},{14,10},{15,13... | collective-permute-start | bytes 589832 | tf_op jit(solution)/shard_map/ppermute | solution.py:49
  28.4 8.0 %collective-permute-start.7 = (bf16[24,4096]{1,0:T(8,128)(2,1)S(1)}, bf16[24,4096]{1,0:T(8,128)(2,1)S(1)}, u32[]{:S(2)}, u32[]{:S(2)}) collective-permute-start(bf16[24,4096]{1,0:T(8,128)(2,1)S(1)} %collective-permute-done.2.refs_0_), channel_id=1, source_target_pairs={{0,1},{1,0},{2,3},{3,2},{4,5},{5,4},{6,7},{7,6},{8,9},{9,8},{10,11... | collective-permute-start | bytes 589832 | tf_op jit(solution)/shard_map/ppermute | solution.py:64
  28.4 7.5 %collective-permute-start.10 = (bf16[24,4096]{1,0:T(8,128)(2,1)S(1)}, bf16[24,4096]{1,0:T(8,128)(2,1)S(1)}, u32[]{:S(2)}, u32[]{:S(2)}) collective-permute-start(bf16[24,4096]{1,0:T(8,128)(2,1)S(1)} %collective-permute-done.6.refs_1_), channel_id=1, source_target_pairs={{0,4},{1,3},{4,8},{5,1},{8,12},{9,5},{12,14},{13,9},{14,10},{15,13... | collective-permute-start | bytes 589832 | tf_op jit(solution)/shard_map/ppermute | solution.py:49
  33.8 5.7 %collective-permute-start.13 = (bf16[24,4096]{1,0:T(8,128)(2,1)S(1)}, bf16[24,4096]{1,0:T(8,128)(2,1)S(1)}, u32[]{:S(2)}, u32[]{:S(2)}) collective-permute-start(bf16[24,4096]{1,0:T(8,128)(2,1)S(1)} %collective-permute-done.9.refs_0_), channel_id=1, source_target_pairs={{0,4},{1,3},{4,8},{5,1},{8,12},{9,5},{12,14},{13,9},{14,10},{15,13... | collective-permute-start | bytes 589832 | tf_op jit(solution)/shard_map/ppermute | solution.py:49
  35.9 3.6 %collective-permute-start.8 = (bf16[24,4096]{1,0:T(8,128)(2,1)S(1)}, bf16[24,4096]{1,0:T(8,128)(2,1)S(1)}, u32[]{:S(2)}, u32[]{:S(2)}) collective-permute-start(bf16[24,4096]{1,0:T(8,128)(2,1)S(1)} %collective-permute-done.6.refs_1_), channel_id=1, source_target_pairs={{0,1},{1,0},{2,3},{3,2},{4,5},{5,4},{6,7},{7,6},{8,9},{9,8},{10,11... | collective-permute-start | bytes 589832 | tf_op jit(solution)/shard_map/ppermute | solution.py:64
  35.9 5.6 %collective-permute-start.12 = (bf16[24,4096]{1,0:T(8,128)(2,1)S(1)}, bf16[24,4096]{1,0:T(8,128)(2,1)S(1)}, u32[]{:S(2)}, u32[]{:S(2)}) collective-permute-start(bf16[24,4096]{1,0:T(8,128)(2,1)S(1)} %collective-permute-done.10.refs_1_), channel_id=1, source_target_pairs={{0,1},{1,0},{2,3},{3,2},{4,5},{5,4},{6,7},{7,6},{8,9},{9,8},{10,11... | collective-permute-start | bytes 589832 | tf_op jit(solution)/shard_map/ppermute | solution.py:64
  36.4 5.1 %collective-permute-start.11 = (bf16[24,4096]{1,0:T(8,128)(2,1)S(1)}, bf16[24,4096]{1,0:T(8,128)(2,1)S(1)}, u32[]{:S(2)}, u32[]{:S(2)}) collective-permute-start(bf16[24,4096]{1,0:T(8,128)(2,1)S(1)} %collective-permute-done.9.refs_0_), channel_id=1, source_target_pairs={{0,1},{1,0},{2,3},{3,2},{4,5},{5,4},{6,7},{7,6},{8,9},{9,8},{10,11... | collective-permute-start | bytes 589832 | tf_op jit(solution)/shard_map/ppermute | solution.py:64
  39.5 2.0 %collective-permute-start.14 = (bf16[24,4096]{1,0:T(8,128)(2,1)S(1)}, bf16[24,4096]{1,0:T(8,128)(2,1)S(1)}, u32[]{:S(2)}, u32[]{:S(2)}) collective-permute-start(bf16[24,4096]{1,0:T(8,128)(2,1)S(1)} %collective-permute-done.13.refs_4_), channel_id=1, source_target_pairs={{0,1},{1,0},{2,3},{3,2},{4,5},{5,4},{6,7},{7,6},{8,9},{9,8},{10,11... | collective-permute-start | bytes 589832 | tf_op jit(solution)/shard_map/ppermute | solution.py:64
  41.5 2.1 %copy-start.1 = (s32[2,32,4]{1,2,0:T(4,128)S(1)}, s32[2,32,4]{1,2,0:T(4,128)}, u32[]{:S(2)}) copy-start(s32[2,32,4]{1,2,0:T(4,128)} %param.27) | copy-start | bytes 3076
  41.5 2.1 %copy-start.2 = (bf16[4,768]{1,0:T(4,128)(2,1)S(1)}, bf16[4,768]{1,0:T(4,128)(2,1)}, u32[]{:S(2)}) copy-start(bf16[4,768]{1,0:T(4,128)(2,1)} %rest_0_.1) | copy-start | bytes 18436
  41.5 2.1 %copy-start.3 = (bf16[768]{0:T(1024)(128)(2,1)S(1)}, bf16[768]{0:T(1024)(128)(2,1)}, u32[]{:S(2)}) copy-start(bf16[768]{0:T(1024)(128)(2,1)} %rest_1_.1) | copy-start | bytes 4612
  41.5 2.1 %copy-start.4 = (bf16[256]{0:T(256)(128)(2,1)S(1)}, bf16[256]{0:T(256)(128)(2,1)}, u32[]{:S(2)}) copy-start(bf16[256]{0:T(256)(128)(2,1)} %rest_2_.1) | copy-start | bytes 1540
  43.6 5.1 %copy-start = (bf16[256,4096]{1,0:T(8,128)(2,1)S(1)}, bf16[256,4096]{1,0:T(8,128)(2,1)}, u32[]{:S(2)}) copy-start(bf16[256,4096]{1,0:T(8,128)(2,1)} %weight_ref.3) | copy-start | bytes 6291460
  48.3 1.8 %collective-permute-start.15 = (bf16[192,256]{1,0:T(8,128)(2,1)S(1)}, bf16[192,256]{1,0:T(8,128)(2,1)S(1)}, u32[]{:S(2)}, u32[]{:S(2)}) collective-permute-start(bf16[192,256]{1,0:T(8,128)(2,1)S(1)} %get-tuple-element.39), channel_id=1, source_target_pairs={{0,1},{1,0},{2,3},{3,2},{4,5},{5,4},{6,7},{7,6},{8,9},{9,8},{10,11... | collective-permute-start | bytes 294920 | tf_op jit(solution)/shard_map/ppermute | solution.py:64
  51.4 5.7 %collective-permute-start.21 = (bf16[24,4096]{1,0:T(8,128)(2,1)S(1)}, bf16[24,4096]{1,0:T(8,128)(2,1)S(1)}, u32[]{:S(2)}, u32[]{:S(2)}) collective-permute-start(bf16[24,4096]{1,0:T(8,128)(2,1)S(1)} %get-tuple-element.42), channel_id=1, source_target_pairs={{0,4},{1,3},{4,8},{5,1},{8,12},{9,5},{12,14},{13,9},{14,10},{15,13... | collective-permute-start | bytes 589832 | tf_op jit(solution)/shard_map/ppermute | solution.py:49
  53.5 5.8 %collective-permute-start.17 = (bf16[24,4096]{1,0:T(8,128)(2,1)S(1)}, bf16[24,4096]{1,0:T(8,128)(2,1)S(1)}, u32[]{:S(2)}, u32[]{:S(2)}) collective-permute-start(bf16[24,4096]{1,0:T(8,128)(2,1)S(1)} %get-tuple-element.41), channel_id=1, source_target_pairs={{0,4},{1,3},{4,8},{5,1},{8,12},{9,5},{12,14},{13,9},{14,10},{15,13... | collective-permute-start | bytes 589832 | tf_op jit(solution)/shard_map/ppermute | solution.py:49
  57.2 5.7 %collective-permute-start.22 = (bf16[24,4096]{1,0:T(8,128)(2,1)S(1)}, bf16[24,4096]{1,0:T(8,128)(2,1)S(1)}, u32[]{:S(2)}, u32[]{:S(2)}) collective-permute-start(bf16[24,4096]{1,0:T(8,128)(2,1)S(1)} %onward.9), channel_id=1, source_target_pairs={{0,4},{1,3},{4,8},{5,1},{8,12},{9,5},{12,14},{13,9},{14,10},{15,13... | collective-permute-start | bytes 589832 | tf_op jit(solution)/shard_map/ppermute | solution.py:49
  59.3 5.7 %collective-permute-start.18 = (bf16[24,4096]{1,0:T(8,128)(2,1)S(1)}, bf16[24,4096]{1,0:T(8,128)(2,1)S(1)}, u32[]{:S(2)}, u32[]{:S(2)}) collective-permute-start(bf16[24,4096]{1,0:T(8,128)(2,1)S(1)} %onward.6), channel_id=1, source_target_pairs={{0,4},{1,3},{4,8},{5,1},{8,12},{9,5},{12,14},{13,9},{14,10},{15,13... | collective-permute-start | bytes 589832 | tf_op jit(solution)/shard_map/ppermute | solution.py:49
  62.9 5.7 %collective-permute-start.23 = (bf16[24,4096]{1,0:T(8,128)(2,1)S(1)}, bf16[24,4096]{1,0:T(8,128)(2,1)S(1)}, u32[]{:S(2)}, u32[]{:S(2)}) collective-permute-start(bf16[24,4096]{1,0:T(8,128)(2,1)S(1)} %onward.10), channel_id=1, source_target_pairs={{0,4},{1,3},{4,8},{5,1},{8,12},{9,5},{12,14},{13,9},{14,10},{15,13... | collective-permute-start | bytes 589832 | tf_op jit(solution)/shard_map/ppermute | solution.py:49
  65.1 5.7 %collective-permute-start.19 = (bf16[24,4096]{1,0:T(8,128)(2,1)S(1)}, bf16[24,4096]{1,0:T(8,128)(2,1)S(1)}, u32[]{:S(2)}, u32[]{:S(2)}) collective-permute-start(bf16[24,4096]{1,0:T(8,128)(2,1)S(1)} %onward.7), channel_id=1, source_target_pairs={{0,4},{1,3},{4,8},{5,1},{8,12},{9,5},{12,14},{13,9},{14,10},{15,13... | collective-permute-start | bytes 589832 | tf_op jit(solution)/shard_map/ppermute | solution.py:49
  68.6 4.9 %collective-permute-start.24 = (bf16[24,4096]{1,0:T(8,128)(2,1)S(1)}, bf16[24,4096]{1,0:T(8,128)(2,1)S(1)}, u32[]{:S(2)}, u32[]{:S(2)}) collective-permute-start(bf16[24,4096]{1,0:T(8,128)(2,1)S(1)} %collective-permute-done.23), channel_id=1, source_target_pairs={{0,1},{1,0},{2,3},{3,2},{4,5},{5,4},{6,7},{7,6},{8,9},{9,8},{10,11... | collective-permute-start | bytes 589832 | tf_op jit(solution)/shard_map/ppermute | solution.py:64
  70.9 5.7 %collective-permute-start.20 = (bf16[24,4096]{1,0:T(8,128)(2,1)S(1)}, bf16[24,4096]{1,0:T(8,128)(2,1)S(1)}, u32[]{:S(2)}, u32[]{:S(2)}) collective-permute-start(bf16[24,4096]{1,0:T(8,128)(2,1)S(1)} %onward.8), channel_id=1, source_target_pairs={{0,4},{1,3},{4,8},{5,1},{8,12},{9,5},{12,14},{13,9},{14,10},{15,13... | collective-permute-start | bytes 589832 | tf_op jit(solution)/shard_map/ppermute | solution.py:49

commit v3 on v2

--- a/solution.py
+++ b/solution.py
@@ -555,7 +555,7 @@
         other_type = stream(other_type, chip_count)
         if step == 2:
             own_type, early = lax.optimization_barrier((own_type, early))
-            staged = [from_hbm(early)]
+            staged = [early]
             received, weight_here, rates_here = lax.optimization_barrier(
                 (received, in_weight, dt_weight)
             )

time: 77.6 us -> 77 us (level)
  no operation moved by 1% of the time
where the time goes in v3:
time: 77 us; the launch traced here: 76.7 us
  starting transfers between devices  33.7 us (44%)
  Pallas kernels  26.3 us (34%)
  waiting for transfers between devices  13.7 us (18%)
  other arithmetic  1.51 us (2%)
  between operations  0.87 us (1%)
    ppermute x13, starting transfers between devices, stream(): return lax.ppermute(array, 'dp', pairs)  24.5 us
    pallas_call x13, Pallas kernels, kernel_call(): pl.pallas_call(kernel, out_shape=outs, in_specs=[scalars] * smem + [whole...  16.2 us
    ppermute x13, waiting for transfers between devices, stream(): return lax.ppermute(array, 'dp', pairs)  12.7 us
    pallas_call x1, Pallas kernels, early_stage(): pl.pallas_call(functools.partial(early_kernel, count, tile), out_shape=pl...  6.77 us
    all_to_all x1, starting transfers between devices, body(): lax.all_to_all(offered, 'dp', split_axis=0, concat_axis=0, tiled=True)  6.32 us
    pallas_call x1, Pallas kernels, load(): pl.pallas_call(load_kernel, out_shape=[jax.ShapeDtypeStruct(a.shape, a.dt...  3.4 us
    ppermute x11, starting transfers between devices, other_core(): lax.ppermute(array, 'dp', [(d, d ^ 1) for d in range(2 * chip_count)])  2.13 us
  transfers between devices with their start and end apart: 26, of which 7 were waited for; matrix products, arithmetic and copies ran while one was open for 3% of the time, Pallas kernels for 32%

profile of v3, /device:TPU:0, one launch (start us, length us, event | category | flops | bytes accessed | tf_op | source)
XLA Modules:
  0.0 76.7 jit_solution(7392116511903699259)
XLA Ops:
  0.6 3.1 %collective-permute-start = (bf16[24,4096]{1,0:T(8,128)(2,1)}, bf16[24,4096]{1,0:T(8,128)(2,1)S(1)}, u32[]{:S(2)}, u32[]{:S(2)}) collective-permute-start(bf16[24,4096]{1,0:T(8,128)(2,1)} %refs_0_.1), channel_id=1, source_target_pairs={{0,4},{1,3},{4,8},{5,1},{8,12},{9,5},{12,14},{13,9},{14,10},{15,13... | collective-permute-start | bytes 589832 | tf_op jit(solution)/shard_map/ppermute | solution.py:49
  3.7 0.7 collective-permute-start.1
  4.4 2.7 %offer_pages.1 = bf16[16,80,128]{2,1,0:T(8,128)(2,1)} custom-call(s32[1]{0:T(128)} %bitcast.my_ref, s32[2,4,32]{2,1,0:T(4,128)} %bitcast.3, bf16[32,32,128]{2,1,0:T(8,128)(2,1)} %state_ref.1, bf16[3,32,96]{2,1,0:T(8,128)(2,1)} %bitcast.5), custom_call_target="tpu_custom_call" | custom-call | bytes 8388608 | tf_op jit(solution)/shard_map/offer_pages/pallas_call | solution.py:71
  7.1 0.7 pad_add_fusion.scalar_ref
  7.9 0.8 pad_maximum_fusion.number_ref
  8.6 0.0 collective-permute-done.refs_2_
  8.7 1.0 %collective-permute-done.1.refs_3_ = bf16[24,4096]{1,0:T(8,128)(2,1)S(1)} collective-permute-done((bf16[24,4096]{1,0:T(8,128)(2,1)}, bf16[24,4096]{1,0:T(8,128)(2,1)S(1)}, u32[]{:S(2)}, u32[]{:S(2)}) %collective-permute-start.1) | collective-permute-done | bytes 196640 | tf_op jit(solution)/shard_map/ppermute | solution.py:60
  9.6 0.1 collective-permute-start.16
  9.7 6.3 %all-to-all-start = ((bf16[16,80,128]{2,1,0:T(8,128)(2,1)}), bf16[16,80,128]{2,1,0:T(8,128)(2,1)S(1)}, u32[]{:S(2)}, u32[]{:S(2)}) async-start(bf16[16,80,128]{2,1,0:T(8,128)(2,1)} %offer_pages.1), calls=%async_computation | async-start | bytes 655360 | tf_op jit(solution)/shard_map/all_to_all | solution.py:547
  16.1 0.4 collective-permute-start.3
  16.5 0.2 collective-permute-start.4
  16.6 0.3 collective-permute-start.5
  17.0 1.7 %collective-permute-start.2 = (bf16[24,4096]{1,0:T(8,128)(2,1)S(1)}, bf16[24,4096]{1,0:T(8,128)(2,1)S(1)}, u32[]{:S(2)}, u32[]{:S(2)}) collective-permute-start(bf16[24,4096]{1,0:T(8,128)(2,1)S(1)} %collective-permute-done.refs_2_), channel_id=1, source_target_pairs={{0,4},{1,3},{4,8},{5,1},{8,12},{9,5},{12,14},{13,9},{14,10},{15,13... | collective-permute-start | bytes 589832 | tf_op jit(solution)/shard_map/ppermute | solution.py:49
  18.6 0.0 collective-permute-done.3.refs_1_
  18.6 1.5 %collective-permute-start.6 = (bf16[24,4096]{1,0:T(8,128)(2,1)S(1)}, bf16[24,4096]{1,0:T(8,128)(2,1)S(1)}, u32[]{:S(2)}, u32[]{:S(2)}) collective-permute-start(bf16[24,4096]{1,0:T(8,128)(2,1)S(1)} %collective-permute-done.1.refs_3_), channel_id=1, source_target_pairs={{0,4},{1,3},{4,8},{5,1},{8,12},{9,5},{12,14},{13,9},{14,10},{15,13... | collective-permute-start | bytes 589832 | tf_op jit(solution)/shard_map/ppermute | solution.py:49
  20.1 0.0 collective-permute-done.4.refs_4_
  20.1 0.0 collective-permute-done.5.refs_5_
  20.1 6.8 %early_stage.1.rest_3_ = f32[144,1152]{1,0:T(8,128)} custom-call(bf16[24,4096]{1,0:T(8,128)(2,1)} %refs_0_.1, bf16[24,4096]{1,0:T(8,128)(2,1)S(1)} %collective-permute-done.3.refs_1_, bf16[24,4096]{1,0:T(8,128)(2,1)S(1)} %collective-permute-done.refs_2_, bf16[24,4096]{1,0:T(8,128)(2,1)S(1)} %collective-permute-done.1.refs_3_, ...), custom_call_target="tpu_custom_call" | custom-call | flops 2147483648 | bytes 8388608 | tf_op jit(solution)/shard_map/early_stage/pallas_call | solution.py:233
  26.9 1.5 %collective-permute-start.9 = (bf16[24,4096]{1,0:T(8,128)(2,1)S(1)}, bf16[24,4096]{1,0:T(8,128)(2,1)S(1)}, u32[]{:S(2)}, u32[]{:S(2)}) collective-permute-start(bf16[24,4096]{1,0:T(8,128)(2,1)S(1)} %collective-permute-done.2.refs_0_), channel_id=1, source_target_pairs={{0,4},{1,3},{4,8},{5,1},{8,12},{9,5},{12,14},{13,9},{14,10},{15,13... | collective-permute-start | bytes 589832 | tf_op jit(solution)/shard_map/ppermute | solution.py:49
  28.4 0.0 collective-permute-start.7
  28.4 0.0 collective-permute-done.6.refs_1_
  28.4 1.9 %collective-permute-start.10 = (bf16[24,4096]{1,0:T(8,128)(2,1)S(1)}, bf16[24,4096]{1,0:T(8,128)(2,1)S(1)}, u32[]{:S(2)}, u32[]{:S(2)}) collective-permute-start(bf16[24,4096]{1,0:T(8,128)(2,1)S(1)} %collective-permute-done.6.refs_1_), channel_id=1, source_target_pairs={{0,4},{1,3},{4,8},{5,1},{8,12},{9,5},{12,14},{13,9},{14,10},{15,13... | collective-permute-start | bytes 589832 | tf_op jit(solution)/shard_map/ppermute | solution.py:49
  30.3 0.0 all-to-all-done.page_ref
  30.4 3.4 %load.1 = (bf16[4096,1024]{1,0:T(8,128)(2,1)S(1)}, bf16[2,4096]{1,0:T(2,128)(2,1)S(1)}) custom-call(bf16[4096,1024]{1,0:T(8,128)(2,1)} %refs_0_.2, bf16[2,4096]{1,0:T(2,128)(2,1)} %refs_1_), custom_call_target="tpu_custom_call" | custom-call | bytes 8388608 | tf_op jit(solution)/shard_map/load/pallas_call | solution.py:142
  33.8 0.0 collective-permute-done.9.refs_0_
  33.8 2.2 %collective-permute-start.13 = (bf16[24,4096]{1,0:T(8,128)(2,1)S(1)}, bf16[24,4096]{1,0:T(8,128)(2,1)S(1)}, u32[]{:S(2)}, u32[]{:S(2)}) collective-permute-start(bf16[24,4096]{1,0:T(8,128)(2,1)S(1)} %collective-permute-done.9.refs_0_), channel_id=1, source_target_pairs={{0,4},{1,3},{4,8},{5,1},{8,12},{9,5},{12,14},{13,9},{14,10},{15,13... | collective-permute-start | bytes 589832 | tf_op jit(solution)/shard_map/ppermute | solution.py:49
  35.9 0.5 collective-permute-start.12
  36.4 0.0 collective-permute-done.7.refs_2_
  36.4 0.1 collective-permute-start.11
  36.5 3.0 %collective-permute-done.13.refs_4_ = bf16[24,4096]{1,0:T(8,128)(2,1)S(1)} collective-permute-done((bf16[24,4096]{1,0:T(8,128)(2,1)S(1)}, bf16[24,4096]{1,0:T(8,128)(2,1)S(1)}, u32[]{:S(2)}, u32[]{:S(2)}) %collective-permute-start.13) | collective-permute-done | bytes 196640 | tf_op jit(solution)/shard_map/ppermute | solution.py:49
  39.5 0.0 collective-permute-start.14
  39.5 0.0 collective-permute-done.8.refs_3_
  39.5 2.0 %stage.2.rest_4_ = f32[96,1152]{1,0:T(8,128)S(1)} custom-call(bf16[24,4096]{1,0:T(8,128)(2,1)S(1)} %collective-permute-done.2.refs_0_, bf16[24,4096]{1,0:T(8,128)(2,1)S(1)} %collective-permute-done.6.refs_1_, bf16[24,4096]{1,0:T(8,128)(2,1)S(1)} %collective-permute-done.7.refs_2_, bf16[24,4096]{1,0:T(8,128)(2,1)S(1)} %collective-permute-done.8.refs_3_, ...), custom_call_target="tpu_custom_call" | custom-call | flops 2415919104 | bytes 8388608 | tf_op jit(solution)/shard_map/stage/pallas_call | solution.py:71
  41.5 0.0 copy-start.2
  41.5 0.0 copy-start.3
  41.5 0.0 copy-start.4
  41.5 0.0 copy-start.5
  41.5 0.0 collective-permute-done.12.refs_3_
  41.5 0.0 collective-permute-done.14.refs_5_
  41.6 2.1 %stage.3.rest_5_ = f32[144,1152]{1,0:T(8,128)S(1)} custom-call(bf16[24,4096]{1,0:T(8,128)(2,1)S(1)} %collective-permute-done.9.refs_0_, bf16[24,4096]{1,0:T(8,128)(2,1)S(1)} %collective-permute-done.10.refs_1_, bf16[24,4096]{1,0:T(8,128)(2,1)S(1)} %collective-permute-done.11.refs_2_, bf16[24,4096]{1,0:T(8,128)(2,1)S(1)} %collective-permute-done.12.refs_3_, ...), custom_call_target="tpu_custom_call" | custom-call | flops 2415919104 | bytes 8388608 | tf_op jit(solution)/shard_map/stage/pallas_call | solution.py:71
  43.7 0.0 copy-start
  43.7 4.0 %mixer.1 = (f32[2,2,128,128]{3,2,1,0:T(8,128)}, bf16[2,3,768]{2,1,0:T(4,128)(2,1)S(1)}, bf16[192,256]{1,0:T(8,128)(2,1)S(1)}, bf16[192,256]{1,0:T(8,128)(2,1)S(1)}) custom-call(s32[19]{0:T(128)S(1)} %pad_add_fusion.scalar_ref, s32[2,4,32]{2,1,0:T(4,128)S(1)} %bitcast.4, f32[6]{0:T(128)S(1)} %pad_maximum_fusion.number_ref, ...), custom_call_target="tpu_custom_call" | custom-call | flops 1073741824 | bytes 8388608 | tf_op jit(solution)/shard_map/mixer/pallas_call | solution.py:71
  47.6 0.5 collective-permute-start.15
  48.2 1.3 %sums_part.1.part_ref = f32[48,4096]{1,0:T(8,128)S(1)} custom-call(bf16[192,256]{1,0:T(8,128)(2,1)S(1)} %get-tuple-element.38.mine_ref, bf16[256,4096]{1,0:T(8,128)(2,1)S(1)} %copy-done), custom_call_target="tpu_custom_call" | custom-call | flops 1073741824 | bytes 8388608 | tf_op jit(solution)/shard_map/sums_part/pallas_call | solution.py:71
  49.4 0.0 collective-permute-done.15.theirs_ref
  49.5 1.3 %sums_first.1 = (bf16[24,4096]{1,0:T(8,128)(2,1)S(1)}, bf16[24,4096]{1,0:T(8,128)(2,1)S(1)}) custom-call(f32[48,4096]{1,0:T(8,128)S(1)} %sums_part.1.part_ref, bf16[192,256]{1,0:T(8,128)(2,1)S(1)} %collective-permute-done.15.theirs_ref, bf16[256,4096]{1,0:T(8,128)(2,1)S(1)} %collective-permute-done.16.held_ref), custom_call_target="tpu_custom_call" | custom-call | flops 1073741824 | bytes 8388608 | tf_op jit(solution)/shard_map/sums_first/pallas_call | solution.py:71
  50.8 2.2 %collective-permute-start.21 = (bf16[24,4096]{1,0:T(8,128)(2,1)S(1)}, bf16[24,4096]{1,0:T(8,128)(2,1)S(1)}, u32[]{:S(2)}, u32[]{:S(2)}) collective-permute-start(bf16[24,4096]{1,0:T(8,128)(2,1)S(1)} %get-tuple-element.42), channel_id=1, source_target_pairs={{0,4},{1,3},{4,8},{5,1},{8,12},{9,5},{12,14},{13,9},{14,10},{15,13... | collective-permute-start | bytes 589832 | tf_op jit(solution)/shard_map/ppermute | solution.py:49
  52.9 0.1 collective-permute-start.17
  53.0 2.0 %sums_rest.1.share_ref = f32[144,4096]{1,0:T(8,128)S(1)} custom-call(bf16[192,256]{1,0:T(8,128)(2,1)S(1)} %get-tuple-element.38.mine_ref, bf16[192,256]{1,0:T(8,128)(2,1)S(1)} %collective-permute-done.15.theirs_ref, bf16[256,4096]{1,0:T(8,128)(2,1)S(1)} %copy-done, bf16[256,4096]{1,0:T(8,128)(2,1)S(1)} %collective-permute-done.16.held_ref), custom_call_target="tpu_custom_call" | custom-call | flops 1073741824 | bytes 8388608 | tf_op jit(solution)/shard_map/sums_rest/pallas_call | solution.py:71
  55.0 1.5 %collective-permute-done.21.refs_0_ = bf16[24,4096]{1,0:T(8,128)(2,1)S(1)} collective-permute-done((bf16[24,4096]{1,0:T(8,128)(2,1)S(1)}, bf16[24,4096]{1,0:T(8,128)(2,1)S(1)}, u32[]{:S(2)}, u32[]{:S(2)}) %collective-permute-start.21) | collective-permute-done | bytes 196640 | tf_op jit(solution)/shard_map/ppermute | solution.py:49
  56.5 2.2 %collective-permute-start.22 = (bf16[24,4096]{1,0:T(8,128)(2,1)S(1)}, bf16[24,4096]{1,0:T(8,128)(2,1)S(1)}, u32[]{:S(2)}, u32[]{:S(2)}) collective-permute-start(bf16[24,4096]{1,0:T(8,128)(2,1)S(1)} %onward.9), channel_id=1, source_target_pairs={{0,4},{1,3},{4,8},{5,1},{8,12},{9,5},{12,14},{13,9},{14,10},{15,13... | collective-permute-start | bytes 589832 | tf_op jit(solution)/shard_map/ppermute | solution.py:49
  58.7 0.0 collective-permute-done.17.refs_0_
  58.7 2.1 %collective-permute-start.18 = (bf16[24,4096]{1,0:T(8,128)(2,1)S(1)}, bf16[24,4096]{1,0:T(8,128)(2,1)S(1)}, u32[]{:S(2)}, u32[]{:S(2)}) collective-permute-start(bf16[24,4096]{1,0:T(8,128)(2,1)S(1)} %onward.6), channel_id=1, source_target_pairs={{0,4},{1,3},{4,8},{5,1},{8,12},{9,5},{12,14},{13,9},{14,10},{15,13... | collective-permute-start | bytes 589832 | tf_op jit(solution)/shard_map/ppermute | solution.py:49
  60.8 1.5 %collective-permute-done.22.refs_0_ = bf16[24,4096]{1,0:T(8,128)(2,1)S(1)} collective-permute-done((bf16[24,4096]{1,0:T(8,128)(2,1)S(1)}, bf16[24,4096]{1,0:T(8,128)(2,1)S(1)}, u32[]{:S(2)}, u32[]{:S(2)}) %collective-permute-start.22) | collective-permute-done | bytes 196640 | tf_op jit(solution)/shard_map/ppermute | solution.py:49
  62.3 2.2 %collective-permute-start.23 = (bf16[24,4096]{1,0:T(8,128)(2,1)S(1)}, bf16[24,4096]{1,0:T(8,128)(2,1)S(1)}, u32[]{:S(2)}, u32[]{:S(2)}) collective-permute-start(bf16[24,4096]{1,0:T(8,128)(2,1)S(1)} %onward.10), channel_id=1, source_target_pairs={{0,4},{1,3},{4,8},{5,1},{8,12},{9,5},{12,14},{13,9},{14,10},{15,13... | collective-permute-start | bytes 589832 | tf_op jit(solution)/shard_map/ppermute | solution.py:49
  64.5 0.0 collective-permute-done.18.refs_0_
  64.5 2.1 %collective-permute-start.19 = (bf16[24,4096]{1,0:T(8,128)(2,1)S(1)}, bf16[24,4096]{1,0:T(8,128)(2,1)S(1)}, u32[]{:S(2)}, u32[]{:S(2)}) collective-permute-start(bf16[24,4096]{1,0:T(8,128)(2,1)S(1)} %onward.7), channel_id=1, source_target_pairs={{0,4},{1,3},{4,8},{5,1},{8,12},{9,5},{12,14},{13,9},{14,10},{15,13... | collective-permute-start | bytes 589832 | tf_op jit(solution)/shard_map/ppermute | solution.py:49
  66.6 1.5 %collective-permute-done.23 = bf16[24,4096]{1,0:T(8,128)(2,1)S(1)} collective-permute-done((bf16[24,4096]{1,0:T(8,128)(2,1)S(1)}, bf16[24,4096]{1,0:T(8,128)(2,1)S(1)}, u32[]{:S(2)}, u32[]{:S(2)}) %collective-permute-start.23) | collective-permute-done | bytes 196640 | tf_op jit(solution)/shard_map/ppermute | solution.py:49
  68.0 0.0 collective-permute-start.24
  68.0 2.2 %collective-permute-done.19.refs_0_ = bf16[24,4096]{1,0:T(8,128)(2,1)S(1)} collective-permute-done((bf16[24,4096]{1,0:T(8,128)(2,1)S(1)}, bf16[24,4096]{1,0:T(8,128)(2,1)S(1)}, u32[]{:S(2)}, u32[]{:S(2)}) %collective-permute-start.19) | collective-permute-done | bytes 196640 | tf_op jit(solution)/shard_map/ppermute | solution.py:49
  70.3 2.1 %collective-permute-start.20 = (bf16[24,4096]{1,0:T(8,128)(2,1)S(1)}, bf16[24,4096]{1,0:T(8,128)(2,1)S(1)}, u32[]{:S(2)}, u32[]{:S(2)}) collective-permute-start(bf16[24,4096]{1,0:T(8,128)(2,1)S(1)} %onward.8), channel_id=1, source_target_pairs={{0,4},{1,3},{4,8},{5,1},{8,12},{9,5},{12,14},{13,9},{14,10},{15,13... | collective-permute-start | bytes 589832 | tf_op jit(solution)/shard_map/ppermute | solution.py:49
  72.3 0.6 copy.18
  72.9 3.0 %collective-permute-done.20.refs_0_ = bf16[24,4096]{1,0:T(8,128)(2,1)S(1)} collective-permute-done((bf16[24,4096]{1,0:T(8,128)(2,1)S(1)}, bf16[24,4096]{1,0:T(8,128)(2,1)S(1)}, u32[]{:S(2)}, u32[]{:S(2)}) %collective-permute-start.20) | collective-permute-done | bytes 196640 | tf_op jit(solution)/shard_map/ppermute | solution.py:49
  76.0 0.7 onward.11
  (18 shorter events, 0.2 us)
Async XLA Ops:
  0.6 8.0 %collective-permute-start = (bf16[24,4096]{1,0:T(8,128)(2,1)}, bf16[24,4096]{1,0:T(8,128)(2,1)S(1)}, u32[]{:S(2)}, u32[]{:S(2)}) collective-permute-start(bf16[24,4096]{1,0:T(8,128)(2,1)} %refs_0_.1), channel_id=1, source_target_pairs={{0,4},{1,3},{4,8},{5,1},{8,12},{9,5},{12,14},{13,9},{14,10},{15,13... | collective-permute-start | bytes 589832 | tf_op jit(solution)/shard_map/ppermute | solution.py:49
  3.7 5.9 %collective-permute-start.1 = (bf16[24,4096]{1,0:T(8,128)(2,1)}, bf16[24,4096]{1,0:T(8,128)(2,1)S(1)}, u32[]{:S(2)}, u32[]{:S(2)}) collective-permute-start(bf16[24,4096]{1,0:T(8,128)(2,1)} %refs_0_.1), channel_id=1, source_target_pairs={{1,4},{0,3},{5,8},{4,1},{9,12},{8,5},{13,14},{12,9},{15,10},{14,13... | collective-permute-start | bytes 589832 | tf_op jit(solution)/shard_map/ppermute | solution.py:60
  9.6 39.8 %collective-permute-start.16 = (bf16[256,4096]{1,0:T(8,128)(2,1)}, bf16[256,4096]{1,0:T(8,128)(2,1)S(1)}, u32[]{:S(2)}, u32[]{:S(2)}) collective-permute-start(bf16[256,4096]{1,0:T(8,128)(2,1)} %weight_ref.3), channel_id=1, source_target_pairs={{0,1},{1,0},{2,3},{3,2},{4,5},{5,4},{6,7},{7,6},{8,9},{9,8},{10,11... | collective-permute-start | bytes 6291464 | tf_op jit(solution)/shard_map/ppermute | solution.py:64
  9.7 20.6 %all-to-all-start = ((bf16[16,80,128]{2,1,0:T(8,128)(2,1)}), bf16[16,80,128]{2,1,0:T(8,128)(2,1)S(1)}, u32[]{:S(2)}, u32[]{:S(2)}) async-start(bf16[16,80,128]{2,1,0:T(8,128)(2,1)} %offer_pages.1), calls=%async_computation | async-start | bytes 655360 | tf_op jit(solution)/shard_map/all_to_all | solution.py:547
  16.1 2.6 %collective-permute-start.3 = (bf16[24,4096]{1,0:T(8,128)(2,1)}, bf16[24,4096]{1,0:T(8,128)(2,1)S(1)}, u32[]{:S(2)}, u32[]{:S(2)}) collective-permute-start(bf16[24,4096]{1,0:T(8,128)(2,1)} %refs_0_.1), channel_id=1, source_target_pairs={{0,1},{1,0},{2,3},{3,2},{4,5},{5,4},{6,7},{7,6},{8,9},{9,8},{10,11... | collective-permute-start | bytes 589832 | tf_op jit(solution)/shard_map/ppermute | solution.py:64
  16.5 3.6 %collective-permute-start.4 = (bf16[24,4096]{1,0:T(8,128)(2,1)S(1)}, bf16[24,4096]{1,0:T(8,128)(2,1)S(1)}, u32[]{:S(2)}, u32[]{:S(2)}) collective-permute-start(bf16[24,4096]{1,0:T(8,128)(2,1)S(1)} %collective-permute-done.refs_2_), channel_id=1, source_target_pairs={{0,1},{1,0},{2,3},{3,2},{4,5},{5,4},{6,7},{7,6},{8,9},{9,8},{10,11... | collective-permute-start | bytes 589832 | tf_op jit(solution)/shard_map/ppermute | solution.py:64
  16.6 3.5 %collective-permute-start.5 = (bf16[24,4096]{1,0:T(8,128)(2,1)S(1)}, bf16[24,4096]{1,0:T(8,128)(2,1)S(1)}, u32[]{:S(2)}, u32[]{:S(2)}) collective-permute-start(bf16[24,4096]{1,0:T(8,128)(2,1)S(1)} %collective-permute-done.1.refs_3_), channel_id=1, source_target_pairs={{0,1},{1,0},{2,3},{3,2},{4,5},{5,4},{6,7},{7,6},{8,9},{9,8},{10,11... | collective-permute-start | bytes 589832 | tf_op jit(solution)/shard_map/ppermute | solution.py:64
  17.0 9.9 %collective-permute-start.2 = (bf16[24,4096]{1,0:T(8,128)(2,1)S(1)}, bf16[24,4096]{1,0:T(8,128)(2,1)S(1)}, u32[]{:S(2)}, u32[]{:S(2)}) collective-permute-start(bf16[24,4096]{1,0:T(8,128)(2,1)S(1)} %collective-permute-done.refs_2_), channel_id=1, source_target_pairs={{0,4},{1,3},{4,8},{5,1},{8,12},{9,5},{12,14},{13,9},{14,10},{15,13... | collective-permute-start | bytes 589832 | tf_op jit(solution)/shard_map/ppermute | solution.py:49
  18.6 9.8 %collective-permute-start.6 = (bf16[24,4096]{1,0:T(8,128)(2,1)S(1)}, bf16[24,4096]{1,0:T(8,128)(2,1)S(1)}, u32[]{:S(2)}, u32[]{:S(2)}) collective-permute-start(bf16[24,4096]{1,0:T(8,128)(2,1)S(1)} %collective-permute-done.1.refs_3_), channel_id=1, source_target_pairs={{0,4},{1,3},{4,8},{5,1},{8,12},{9,5},{12,14},{13,9},{14,10},{15,13... | collective-permute-start | bytes 589832 | tf_op jit(solution)/shard_map/ppermute | solution.py:49
  26.9 6.9 %collective-permute-start.9 = (bf16[24,4096]{1,0:T(8,128)(2,1)S(1)}, bf16[24,4096]{1,0:T(8,128)(2,1)S(1)}, u32[]{:S(2)}, u32[]{:S(2)}) collective-permute-start(bf16[24,4096]{1,0:T(8,128)(2,1)S(1)} %collective-permute-done.2.refs_0_), channel_id=1, source_target_pairs={{0,4},{1,3},{4,8},{5,1},{8,12},{9,5},{12,14},{13,9},{14,10},{15,13... | collective-permute-start | bytes 589832 | tf_op jit(solution)/shard_map/ppermute | solution.py:49
  28.4 8.0 %collective-permute-start.7 = (bf16[24,4096]{1,0:T(8,128)(2,1)S(1)}, bf16[24,4096]{1,0:T(8,128)(2,1)S(1)}, u32[]{:S(2)}, u32[]{:S(2)}) collective-permute-start(bf16[24,4096]{1,0:T(8,128)(2,1)S(1)} %collective-permute-done.2.refs_0_), channel_id=1, source_target_pairs={{0,1},{1,0},{2,3},{3,2},{4,5},{5,4},{6,7},{7,6},{8,9},{9,8},{10,11... | collective-permute-start | bytes 589832 | tf_op jit(solution)/shard_map/ppermute | solution.py:64
  28.4 7.5 %collective-permute-start.10 = (bf16[24,4096]{1,0:T(8,128)(2,1)S(1)}, bf16[24,4096]{1,0:T(8,128)(2,1)S(1)}, u32[]{:S(2)}, u32[]{:S(2)}) collective-permute-start(bf16[24,4096]{1,0:T(8,128)(2,1)S(1)} %collective-permute-done.6.refs_1_), channel_id=1, source_target_pairs={{0,4},{1,3},{4,8},{5,1},{8,12},{9,5},{12,14},{13,9},{14,10},{15,13... | collective-permute-start | bytes 589832 | tf_op jit(solution)/shard_map/ppermute | solution.py:49
  33.8 5.7 %collective-permute-start.13 = (bf16[24,4096]{1,0:T(8,128)(2,1)S(1)}, bf16[24,4096]{1,0:T(8,128)(2,1)S(1)}, u32[]{:S(2)}, u32[]{:S(2)}) collective-permute-start(bf16[24,4096]{1,0:T(8,128)(2,1)S(1)} %collective-permute-done.9.refs_0_), channel_id=1, source_target_pairs={{0,4},{1,3},{4,8},{5,1},{8,12},{9,5},{12,14},{13,9},{14,10},{15,13... | collective-permute-start | bytes 589832 | tf_op jit(solution)/shard_map/ppermute | solution.py:49
  35.9 3.6 %collective-permute-start.8 = (bf16[24,4096]{1,0:T(8,128)(2,1)S(1)}, bf16[24,4096]{1,0:T(8,128)(2,1)S(1)}, u32[]{:S(2)}, u32[]{:S(2)}) collective-permute-start(bf16[24,4096]{1,0:T(8,128)(2,1)S(1)} %collective-permute-done.6.refs_1_), channel_id=1, source_target_pairs={{0,1},{1,0},{2,3},{3,2},{4,5},{5,4},{6,7},{7,6},{8,9},{9,8},{10,11... | collective-permute-start | bytes 589832 | tf_op jit(solution)/shard_map/ppermute | solution.py:64
  35.9 5.6 %collective-permute-start.12 = (bf16[24,4096]{1,0:T(8,128)(2,1)S(1)}, bf16[24,4096]{1,0:T(8,128)(2,1)S(1)}, u32[]{:S(2)}, u32[]{:S(2)}) collective-permute-start(bf16[24,4096]{1,0:T(8,128)(2,1)S(1)} %collective-permute-done.10.refs_1_), channel_id=1, source_target_pairs={{0,1},{1,0},{2,3},{3,2},{4,5},{5,4},{6,7},{7,6},{8,9},{9,8},{10,11... | collective-permute-start | bytes 589832 | tf_op jit(solution)/shard_map/ppermute | solution.py:64
  36.4 5.1 %collective-permute-start.11 = (bf16[24,4096]{1,0:T(8,128)(2,1)S(1)}, bf16[24,4096]{1,0:T(8,128)(2,1)S(1)}, u32[]{:S(2)}, u32[]{:S(2)}) collective-permute-start(bf16[24,4096]{1,0:T(8,128)(2,1)S(1)} %collective-permute-done.9.refs_0_), channel_id=1, source_target_pairs={{0,1},{1,0},{2,3},{3,2},{4,5},{5,4},{6,7},{7,6},{8,9},{9,8},{10,11... | collective-permute-start | bytes 589832 | tf_op jit(solution)/shard_map/ppermute | solution.py:64
  39.5 2.1 %collective-permute-start.14 = (bf16[24,4096]{1,0:T(8,128)(2,1)S(1)}, bf16[24,4096]{1,0:T(8,128)(2,1)S(1)}, u32[]{:S(2)}, u32[]{:S(2)}) collective-permute-start(bf16[24,4096]{1,0:T(8,128)(2,1)S(1)} %collective-permute-done.13.refs_4_), channel_id=1, source_target_pairs={{0,1},{1,0},{2,3},{3,2},{4,5},{5,4},{6,7},{7,6},{8,9},{9,8},{10,11... | collective-permute-start | bytes 589832 | tf_op jit(solution)/shard_map/ppermute | solution.py:64
  41.5 2.2 %copy-start.1 = (f32[144,1152]{1,0:T(8,128)S(1)}, f32[144,1152]{1,0:T(8,128)}, u32[]{:S(2)}) copy-start(f32[144,1152]{1,0:T(8,128)} %early_stage.1.rest_3_) | copy-start | bytes 1990660
  41.5 2.2 %copy-start.2 = (s32[2,32,4]{1,2,0:T(4,128)S(1)}, s32[2,32,4]{1,2,0:T(4,128)}, u32[]{:S(2)}) copy-start(s32[2,32,4]{1,2,0:T(4,128)} %param.27) | copy-start | bytes 3076
  41.5 2.1 %copy-start.3 = (bf16[4,768]{1,0:T(4,128)(2,1)S(1)}, bf16[4,768]{1,0:T(4,128)(2,1)}, u32[]{:S(2)}) copy-start(bf16[4,768]{1,0:T(4,128)(2,1)} %rest_0_.1) | copy-start | bytes 18436
  41.5 2.1 %copy-start.4 = (bf16[768]{0:T(1024)(128)(2,1)S(1)}, bf16[768]{0:T(1024)(128)(2,1)}, u32[]{:S(2)}) copy-start(bf16[768]{0:T(1024)(128)(2,1)} %rest_1_.1) | copy-start | bytes 4612
  41.5 2.1 %copy-start.5 = (bf16[256]{0:T(256)(128)(2,1)S(1)}, bf16[256]{0:T(256)(128)(2,1)}, u32[]{:S(2)}) copy-start(bf16[256]{0:T(256)(128)(2,1)} %rest_2_.1) | copy-start | bytes 1540
  43.7 4.5 %copy-start = (bf16[256,4096]{1,0:T(8,128)(2,1)S(1)}, bf16[256,4096]{1,0:T(8,128)(2,1)}, u32[]{:S(2)}) copy-start(bf16[256,4096]{1,0:T(8,128)(2,1)} %weight_ref.3) | copy-start | bytes 6291460
  47.6 1.8 %collective-permute-start.15 = (bf16[192,256]{1,0:T(8,128)(2,1)S(1)}, bf16[192,256]{1,0:T(8,128)(2,1)S(1)}, u32[]{:S(2)}, u32[]{:S(2)}) collective-permute-start(bf16[192,256]{1,0:T(8,128)(2,1)S(1)} %get-tuple-element.39), channel_id=1, source_target_pairs={{0,1},{1,0},{2,3},{3,2},{4,5},{5,4},{6,7},{7,6},{8,9},{9,8},{10,11... | collective-permute-start | bytes 294920 | tf_op jit(solution)/shard_map/ppermute | solution.py:64
  50.8 5.7 %collective-permute-start.21 = (bf16[24,4096]{1,0:T(8,128)(2,1)S(1)}, bf16[24,4096]{1,0:T(8,128)(2,1)S(1)}, u32[]{:S(2)}, u32[]{:S(2)}) collective-permute-start(bf16[24,4096]{1,0:T(8,128)(2,1)S(1)} %get-tuple-element.42), channel_id=1, source_target_pairs={{0,4},{1,3},{4,8},{5,1},{8,12},{9,5},{12,14},{13,9},{14,10},{15,13... | collective-permute-start | bytes 589832 | tf_op jit(solution)/shard_map/ppermute | solution.py:49
  52.9 5.8 %collective-permute-start.17 = (bf16[24,4096]{1,0:T(8,128)(2,1)S(1)}, bf16[24,4096]{1,0:T(8,128)(2,1)S(1)}, u32[]{:S(2)}, u32[]{:S(2)}) collective-permute-start(bf16[24,4096]{1,0:T(8,128)(2,1)S(1)} %get-tuple-element.41), channel_id=1, source_target_pairs={{0,4},{1,3},{4,8},{5,1},{8,12},{9,5},{12,14},{13,9},{14,10},{15,13... | collective-permute-start | bytes 589832 | tf_op jit(solution)/shard_map/ppermute | solution.py:49
  56.5 5.7 %collective-permute-start.22 = (bf16[24,4096]{1,0:T(8,128)(2,1)S(1)}, bf16[24,4096]{1,0:T(8,128)(2,1)S(1)}, u32[]{:S(2)}, u32[]{:S(2)}) collective-permute-start(bf16[24,4096]{1,0:T(8,128)(2,1)S(1)} %onward.9), channel_id=1, source_target_pairs={{0,4},{1,3},{4,8},{5,1},{8,12},{9,5},{12,14},{13,9},{14,10},{15,13... | collective-permute-start | bytes 589832 | tf_op jit(solution)/shard_map/ppermute | solution.py:49
  58.7 5.7 %collective-permute-start.18 = (bf16[24,4096]{1,0:T(8,128)(2,1)S(1)}, bf16[24,4096]{1,0:T(8,128)(2,1)S(1)}, u32[]{:S(2)}, u32[]{:S(2)}) collective-permute-start(bf16[24,4096]{1,0:T(8,128)(2,1)S(1)} %onward.6), channel_id=1, source_target_pairs={{0,4},{1,3},{4,8},{5,1},{8,12},{9,5},{12,14},{13,9},{14,10},{15,13... | collective-permute-start | bytes 589832 | tf_op jit(solution)/shard_map/ppermute | solution.py:49
  62.3 5.7 %collective-permute-start.23 = (bf16[24,4096]{1,0:T(8,128)(2,1)S(1)}, bf16[24,4096]{1,0:T(8,128)(2,1)S(1)}, u32[]{:S(2)}, u32[]{:S(2)}) collective-permute-start(bf16[24,4096]{1,0:T(8,128)(2,1)S(1)} %onward.10), channel_id=1, source_target_pairs={{0,4},{1,3},{4,8},{5,1},{8,12},{9,5},{12,14},{13,9},{14,10},{15,13... | collective-permute-start | bytes 589832 | tf_op jit(solution)/shard_map/ppermute | solution.py:49
  64.5 5.7 %collective-permute-start.19 = (bf16[24,4096]{1,0:T(8,128)(2,1)S(1)}, bf16[24,4096]{1,0:T(8,128)(2,1)S(1)}, u32[]{:S(2)}, u32[]{:S(2)}) collective-permute-start(bf16[24,4096]{1,0:T(8,128)(2,1)S(1)} %onward.7), channel_id=1, source_target_pairs={{0,4},{1,3},{4,8},{5,1},{8,12},{9,5},{12,14},{13,9},{14,10},{15,13... | collective-permute-start | bytes 589832 | tf_op jit(solution)/shard_map/ppermute | solution.py:49
  68.0 4.9 %collective-permute-start.24 = (bf16[24,4096]{1,0:T(8,128)(2,1)S(1)}, bf16[24,4096]{1,0:T(8,128)(2,1)S(1)}, u32[]{:S(2)}, u32[]{:S(2)}) collective-permute-start(bf16[24,4096]{1,0:T(8,128)(2,1)S(1)} %collective-permute-done.23), channel_id=1, source_target_pairs={{0,1},{1,0},{2,3},{3,2},{4,5},{5,4},{6,7},{7,6},{8,9},{9,8},{10,11... | collective-permute-start | bytes 589832 | tf_op jit(solution)/shard_map/ppermute | solution.py:64
  70.3 5.7 %collective-permute-start.20 = (bf16[24,4096]{1,0:T(8,128)(2,1)S(1)}, bf16[24,4096]{1,0:T(8,128)(2,1)S(1)}, u32[]{:S(2)}, u32[]{:S(2)}) collective-permute-start(bf16[24,4096]{1,0:T(8,128)(2,1)S(1)} %onward.8), channel_id=1, source_target_pairs={{0,4},{1,3},{4,8},{5,1},{8,12},{9,5},{12,14},{13,9},{14,10},{15,13... | collective-permute-start | bytes 589832 | tf_op jit(solution)/shard_map/ppermute | solution.py:49
